TPU v7x, 32 devices: a whole 2x2x4 slice. The times are simulated.
32 devices in a mesh: wide: 8 (over z, x), narrow: 4 (over y, core).
Axes of the slice: x: 2, y: 2, z: 4, core: 2. Of those that a mesh axis runs over, the one named last changes fastest.
Arguments:
- cells_in: bfloat16 [2, 8, 1024, 1120], P(None, 'wide', 'narrow'), may hold values from -6 to 6
- lengths: int32 [2, 8], P(None, 'wide'), may hold values from 128 to 1024, as said below
- w_qkv: bfloat16 [60, 62720], P('narrow', 'wide'), may hold values from -0.25 to 0.25
- w_out: bfloat16 [20, 62720], P('narrow', 'wide'), may hold values from -0.75 to 0.75
- w_up: bfloat16 [560, 8960], P('narrow', 'wide'), may hold values from -0.1875 to 0.1875
- w_down: bfloat16 [560, 8960], P('narrow', 'wide'), may hold values from -0.09375 to 0.09375
- ln1_gain: float32 [1120], replicated, may hold values from 0.1 to 1.9
- ln1_shift: float32 [1120], replicated, may hold values from -1.5 to 1.5
- bias_qv: float32 [2240], replicated, may hold values from -1.5 to 1.5
- bias_out: float32 [1120], replicated, may hold values from -1.5 to 1.5
- ln2_gain: float32 [1120], replicated, may hold values from 0.1 to 1.9
- ln2_shift: float32 [1120], replicated, may hold values from -1.5 to 1.5
- bias_up: float32 [4480], replicated, may hold values from -2.5 to 2.5
- bias_down: float32 [1120], replicated, may hold values from -1.5 to 1.5
- cotangent: bfloat16 [2, 8, 1024, 1120], P(None, 'wide', 'narrow'), may hold values from -8 to 8
Outputs:
- cells_out: bfloat16 [2, 8, 1024, 1120], P(None, 'wide', 'narrow')
- grad_in: bfloat16 [2, 8, 1024, 1120], P(None, 'wide', 'narrow')
- grad_qkv: float32 [60, 62720], P('narrow', 'wide')
- grad_out: float32 [20, 62720], P('narrow', 'wide')
- grad_up: float32 [560, 8960], P('narrow', 'wide')
- grad_down: float32 [560, 8960], P('narrow', 'wide')
- grad_ln1_gain: float32 [1120], replicated
- grad_ln1_shift: float32 [1120], replicated
- grad_bias_qv: float32 [2240], replicated
- grad_bias_out: float32 [1120], replicated
- grad_ln2_gain: float32 [1120], replicated
- grad_ln2_shift: float32 [1120], replicated
- grad_bias_up: float32 [4480], replicated
- grad_bias_down: float32 [1120], replicated
Inputs may be any that keep to these rules, and one draw needn't show every extreme that they name: For every cell column c, one of the 2 micro-batches has lengths[b, c] = 1024.
All inputs are finite; a program needn't handle non-finite values.
Results may differ from a plain program's by a relative error of at most 0.013.
Values may be sent and summed in bfloat16 or wider, within the bound.
A program may use at most 320 MiB of HBM per device.

v0:
```python
import jax
import jax.numpy as jnp
from jax import lax
from jax.sharding import PartitionSpec as P

HEAD_DIM = 56
MB = 2


norm_eps = 1e-05


def layer_norm(values, scale_vec, shift_vec):
    center = values - jnp.mean(values, axis=-1, keepdims=True)
    spread = jnp.mean(center * center, axis=-1, keepdims=True)
    return center * lax.rsqrt(spread + norm_eps) * scale_vec + shift_vec


def smooth_gate(values):
    return jax.nn.gelu(values, approximate=True)


def visible(row_start, block_rows, key_count, cell_len):
    query_pos = row_start + jnp.arange(block_rows, dtype=jnp.int32)[:, None]
    key_pos = jnp.arange(key_count, dtype=jnp.int32)[None, :]
    return (key_pos <= query_pos) & (key_pos < cell_len)


def block_scores(queries, key_rows, allowed):
    scores = jnp.einsum(
        "qhe,khe->hqk", queries, key_rows, preferred_element_type=jnp.float32
    ) * HEAD_DIM ** (-0.5)
    return jnp.where(allowed[None], scores, -1e30)


def attend(queries, key_rows, value_rows, cell_len):
    seq_total = queries.shape[0]
    block_rows = min(512, seq_total)
    out_blocks = []
    log_sums = []
    for row_start in range(0, seq_total, block_rows):
        row_end = row_start + block_rows
        allowed = visible(row_start, block_rows, row_end, cell_len)
        scores = block_scores(queries[row_start:row_end], key_rows[:row_end], allowed)
        row_max = jnp.max(scores, axis=-1, keepdims=True)
        weights = jnp.exp(scores - row_max)
        row_total = jnp.sum(weights, axis=-1, keepdims=True)
        probs_low = (weights / row_total).astype(jnp.bfloat16)
        out_blocks.append(
            jnp.einsum(
                "hqk,khe->qhe", probs_low, value_rows[:row_end], preferred_element_type=jnp.float32
            ).astype(jnp.bfloat16)
        )
        log_sums.append(row_max + jnp.log(row_total))
    return (jnp.concatenate(out_blocks, axis=0), log_sums)


def attend_back(queries, key_rows, value_rows, grad_rows, cell_len, log_sums):
    seq_total = queries.shape[0]
    block_rows = min(512, seq_total)
    score_scale = HEAD_DIM ** (-0.5)
    grad_query_blocks = []
    grad_keys = jnp.zeros(key_rows.shape, jnp.float32)
    grad_values = jnp.zeros(value_rows.shape, jnp.float32)
    for block_num, row_start in enumerate(range(0, seq_total, block_rows)):
        row_end = row_start + block_rows
        allowed = visible(row_start, block_rows, row_end, cell_len)
        query_block = queries[row_start:row_end]
        grad_block = grad_rows[row_start:row_end]
        key_part = key_rows[:row_end]
        scores = block_scores(query_block, key_part, allowed)
        probs = jnp.exp(scores - log_sums[block_num])
        probs_low = probs.astype(jnp.bfloat16)
        grad_values = grad_values.at[:row_end].add(
            jnp.einsum("hqk,qhe->khe", probs_low, grad_block, preferred_element_type=jnp.float32)
        )
        grad_probs = jnp.einsum(
            "qhe,khe->hqk", grad_block, value_rows[:row_end], preferred_element_type=jnp.float32
        )
        row_inner = jnp.sum(probs * grad_probs, axis=-1, keepdims=True)
        grad_scores = (probs * (grad_probs - row_inner)).astype(jnp.bfloat16)
        grad_query_blocks.append(
            jnp.einsum("hqk,khe->qhe", grad_scores, key_part, preferred_element_type=jnp.float32)
            * score_scale
        )
        grad_keys = grad_keys.at[:row_end].add(
            jnp.einsum("hqk,qhe->khe", grad_scores, query_block, preferred_element_type=jnp.float32)
            * score_scale
        )
    return (jnp.concatenate(grad_query_blocks, axis=0), grad_keys, grad_values)


def gather_batch(shards):
    columns = (
        lax.all_gather(shards[0], "wide", axis=1, tiled=True),
        lax.all_gather(shards[1], "wide", axis=1, tiled=True),
        lax.all_gather(shards[2], "wide", axis=1, tiled=True),
        lax.all_gather(shards[3], "wide", axis=1, tiled=True),
    )
    return (
        lax.all_gather(columns[0], "narrow", axis=0, tiled=True),
        lax.all_gather(columns[1], "narrow", axis=0, tiled=True),
        lax.all_gather(columns[2], "narrow", axis=0, tiled=True),
        lax.all_gather(columns[3], "narrow", axis=0, tiled=True),
    )


def on_device(
    cells_in,
    lengths,
    w_qkv,
    w_out,
    w_up,
    w_down,
    ln1_gain,
    ln1_shift,
    bias_qv,
    bias_out,
    ln2_gain,
    ln2_shift,
    bias_up,
    bias_down,
    cotangent,
):
    groups = lax.axis_size("narrow")
    local_rows = cells_in.shape[2]
    seq_total = local_rows * groups
    width = cells_in.shape[3]
    heads_total = width // HEAD_DIM
    heads_here = heads_total // groups
    head_width = heads_here * HEAD_DIM
    hidden_width = bias_up.shape[0]
    ff_here = hidden_width // groups
    shard_set = (w_qkv, w_out, w_up, w_down)
    bias_query = bias_qv[:width].reshape(heads_total, 1, HEAD_DIM)
    bias_value = bias_qv[width:].reshape(heads_total, 1, HEAD_DIM)
    qkv_bias = jnp.concatenate(
        [bias_query, jnp.zeros((heads_total, 1, HEAD_DIM), jnp.float32), bias_value], axis=1
    ).reshape(-1)
    grad_store = (
        jnp.zeros((heads_here * 3, HEAD_DIM * width), jnp.float32),
        jnp.zeros((heads_here, HEAD_DIM * width), jnp.float32),
        jnp.zeros((ff_here // 8, 8 * width), jnp.float32),
        jnp.zeros((ff_here // 8, 8 * width), jnp.float32),
    )
    small_store = (
        jnp.zeros((width,), jnp.float32),
        jnp.zeros((width,), jnp.float32),
        jnp.zeros((2 * width,), jnp.float32),
        jnp.zeros((width,), jnp.float32),
        jnp.zeros((width,), jnp.float32),
        jnp.zeros((width,), jnp.float32),
        jnp.zeros((hidden_width,), jnp.float32),
        jnp.zeros((width,), jnp.float32),
    )
    out_list = []
    grad_list = []
    for batch_num in range(MB):
        cell_rows = cells_in[batch_num, 0].astype(jnp.float32)
        cell_len = lengths[batch_num, 0]
        full_weights = gather_batch(shard_set)
        qkv_rows = full_weights[0].reshape(3 * width, width)
        out_mat = full_weights[1].reshape(width, width)
        up_rows = full_weights[2].reshape(hidden_width, width)
        down_mat = full_weights[3].reshape(hidden_width, width)
        normed, norm1_back = jax.vjp(layer_norm, cell_rows, ln1_gain, ln1_shift)
        normed_low = normed.astype(jnp.bfloat16)
        qkv_low = (
            jnp.einsum("td,cd->tc", normed_low, qkv_rows, preferred_element_type=jnp.float32)
            + qkv_bias
        ).astype(jnp.bfloat16)
        head_input = lax.all_to_all(
            qkv_low.reshape(local_rows, groups, 3 * head_width),
            "narrow",
            split_axis=1,
            concat_axis=0,
            tiled=True,
        )
        head_input = head_input.reshape(seq_total, heads_here, 3, HEAD_DIM)
        queries = head_input[:, :, 0]
        key_rows = head_input[:, :, 1]
        value_rows = head_input[:, :, 2]
        head_output, log_sums = attend(queries, key_rows, value_rows, cell_len)
        head_flat = head_output.reshape(seq_total, head_width)
        mixed_low = lax.all_to_all(
            head_flat.reshape(seq_total, 1, head_width),
            "narrow",
            split_axis=0,
            concat_axis=1,
            tiled=True,
        ).reshape(local_rows, width)
        middle = (
            cell_rows + jnp.dot(mixed_low, out_mat, preferred_element_type=jnp.float32) + bias_out
        )
        normed2, norm2_back = jax.vjp(layer_norm, middle, ln2_gain, ln2_shift)
        normed2_low = normed2.astype(jnp.bfloat16)
        upper = (
            jnp.einsum("td,fd->tf", normed2_low, up_rows, preferred_element_type=jnp.float32)
            + bias_up
        )
        hidden, gate_back = jax.vjp(smooth_gate, upper)
        hidden_low = hidden.astype(jnp.bfloat16)
        out_list.append(
            (
                middle
                + jnp.dot(hidden_low, down_mat, preferred_element_type=jnp.float32)
                + bias_down
            ).astype(jnp.bfloat16)
        )
        grad_top_low = cotangent[batch_num, 0]
        grad_top = grad_top_low.astype(jnp.float32)
        normed_all, normed2_all, grad_top_all = (
            lax.all_gather(normed_low, "narrow", axis=0, tiled=True),
            lax.all_gather(normed2_low, "narrow", axis=0, tiled=True),
            lax.all_gather(grad_top_low, "narrow", axis=0, tiled=True),
        )
        grad_hidden = jnp.einsum(
            "td,fd->tf", grad_top_low, down_mat, preferred_element_type=jnp.float32
        )
        grad_upper_low = gate_back(grad_hidden)[0].astype(jnp.bfloat16)
        hidden_cols, grad_upper_cols = (
            lax.all_to_all(
                hidden_low.reshape(local_rows, groups, ff_here),
                "narrow",
                split_axis=1,
                concat_axis=0,
                tiled=True,
            ),
            lax.all_to_all(
                grad_upper_low.reshape(local_rows, groups, ff_here),
                "narrow",
                split_axis=1,
                concat_axis=0,
                tiled=True,
            ),
        )
        hidden_cols = hidden_cols.reshape(seq_total, ff_here)
        grad_upper_cols = grad_upper_cols.reshape(seq_total, ff_here)
        grad_down_here = jnp.einsum(
            "tf,td->fd", hidden_cols, grad_top_all, preferred_element_type=jnp.float32
        ).reshape(ff_here // 8, 8 * width)
        grad_up_here = jnp.einsum(
            "tf,td->fd", grad_upper_cols, normed2_all, preferred_element_type=jnp.float32
        ).reshape(ff_here // 8, 8 * width)
        grad_normed2 = jnp.dot(grad_upper_low, up_rows, preferred_element_type=jnp.float32)
        grad_mid_norm, grad_gain2, grad_shift2 = norm2_back(grad_normed2)
        grad_middle = grad_top + grad_mid_norm
        grad_att_low = grad_middle.astype(jnp.bfloat16)
        grad_att_whole = lax.all_gather(grad_att_low, "narrow", axis=0, tiled=True)
        grad_out_here = jnp.einsum(
            "tc,td->cd", head_flat, grad_att_whole, preferred_element_type=jnp.float32
        ).reshape(heads_here, HEAD_DIM * width)
        grad_mixed_low = jnp.einsum(
            "te,de->td", grad_att_low, out_mat, preferred_element_type=jnp.float32
        ).astype(jnp.bfloat16)
        grad_head_rows = lax.all_to_all(
            grad_mixed_low.reshape(local_rows, groups, head_width),
            "narrow",
            split_axis=1,
            concat_axis=0,
            tiled=True,
        )
        grad_head_rows = grad_head_rows.reshape(seq_total, heads_here, HEAD_DIM)
        grad_q, grad_k, grad_v = attend_back(
            queries, key_rows, value_rows, grad_head_rows, cell_len, log_sums
        )
        grad_stack = (
            jnp.stack([grad_q, grad_k, grad_v], axis=2)
            .astype(jnp.bfloat16)
            .reshape(seq_total, 3 * head_width)
        )
        grad_qkv_here = jnp.einsum(
            "tc,td->cd", grad_stack, normed_all, preferred_element_type=jnp.float32
        ).reshape(heads_here * 3, HEAD_DIM * width)
        grad_qkv_low = lax.all_to_all(
            grad_stack.reshape(seq_total, 1, 3 * head_width),
            "narrow",
            split_axis=0,
            concat_axis=1,
            tiled=True,
        ).reshape(local_rows, 3 * width)
        grad_normed = jnp.dot(grad_qkv_low, qkv_rows, preferred_element_type=jnp.float32)
        grad_cell_norm, grad_gain1, grad_shift1 = norm1_back(grad_normed)
        grad_list.append((grad_middle + grad_cell_norm).astype(jnp.bfloat16))
        grad_qkv_sums = jnp.sum(grad_qkv_low.astype(jnp.float32), axis=0).reshape(
            heads_total, 3, HEAD_DIM
        )
        batch_small = (
            grad_gain1,
            grad_shift1,
            jnp.concatenate([grad_qkv_sums[:, 0].reshape(-1), grad_qkv_sums[:, 2].reshape(-1)]),
            jnp.sum(grad_att_low.astype(jnp.float32), axis=0),
            grad_gain2,
            grad_shift2,
            jnp.sum(grad_upper_low.astype(jnp.float32), axis=0),
            jnp.sum(grad_top, axis=0),
        )
        small_store = tuple((older + newer for older, newer in zip(small_store, batch_small)))
        batch_grads = (grad_qkv_here, grad_out_here, grad_up_here, grad_down_here)
        grad_store = tuple((older + newer for older, newer in zip(grad_store, batch_grads)))
    grad_store = lax.psum_scatter(grad_store, "wide", scatter_dimension=1, tiled=True)
    small_totals = lax.psum(small_store, ("wide", "narrow"))
    cells_out = jnp.stack(out_list, axis=0)[:, None]
    grad_in = jnp.stack(grad_list, axis=0)[:, None]
    return (
        cells_out,
        grad_in,
        grad_store[0],
        grad_store[1],
        grad_store[2],
        grad_store[3],
        small_totals[0],
        small_totals[1],
        small_totals[2],
        small_totals[3],
        small_totals[4],
        small_totals[5],
        small_totals[6],
        small_totals[7],
    )


def solution(mesh):
    return jax.shard_map(
        on_device,
        mesh=mesh,
        in_specs=(
            P(None, "wide", "narrow", None),
            P(None, "wide"),
            P("narrow", "wide"),
            P("narrow", "wide"),
            P("narrow", "wide"),
            P("narrow", "wide"),
            P(),
            P(),
            P(),
            P(),
            P(),
            P(),
            P(),
            P(),
            P(None, "wide", "narrow", None),
        ),
        out_specs=(
            P(None, "wide", "narrow", None),
            P(None, "wide", "narrow", None),
            P("narrow", "wide"),
            P("narrow", "wide"),
            P("narrow", "wide"),
            P("narrow", "wide"),
            P(),
            P(),
            P(),
            P(),
            P(),
            P(),
            P(),
            P(),
        ),
        check_vma=False,
    )
```

profile of v0, /device:TPU:0, one launch (start us, length us, event | category | flops | bytes accessed | tf_op | source)
XLA Modules:
  0.0 2168.5 jit_solution(5646274235735630230)
XLA Ops:
  9.4 52.0 %all-gather.42.cloned.1.call-done = bf16[8,7840,15]{1,2,0:T(8,128)(2,1)} async-done(((bf16[1,7840,15]{1,2,0:T(8,128)(2,1)}), bf16[8,7840,15]{1,2,0:T(8,128)(2,1)}) %all-gather.42.cloned.1.call-update) | async-done | bytes 1881616 | tf_op jit(solution)/shard_map/all_gather | solution.py:95
  67.8 34.2 %all-gather.4 = bf16[8,7840,5]{1,2,0:T(8,128)(2,1)S(1)} all-gather(bf16[1,7840,5]{1,2,0:T(8,128)(2,1)S(1)} %bitcast.501), channel_id=1, replica_groups=mesh['wide'=8,'narrow'=4] {'wide'}, dimensions={0}, use_global_device_ids=true | all-gather | bytes 705600 | tf_op jit(solution)/shard_map/all_gather | solution.py:96
  104.2 20.7 all-gather.48.cloned.1.call-done
  136.6 44.7 %all-gather.52.cloned.1.call-done = bf16[8,1120,140]{1,2,0:T(8,128)(2,1)} async-done(((bf16[1,1120,140]{1,2,0:T(8,128)(2,1)}), bf16[8,1120,140]{1,2,0:T(8,128)(2,1)}) %all-gather.52.cloned.1.call-update) | async-done | bytes 2508816 | tf_op jit(solution)/shard_map/all_gather | solution.py:98
  190.7 46.9 %all-gather.44.cloned.1.call-done = bf16[4,15,62720]{2,1,0:T(8,128)(2,1)} async-done(((bf16[1,15,62720]{2,1,0:T(8,128)(2,1)}), bf16[4,15,62720]{2,1,0:T(8,128)(2,1)}) %all-gather.44.cloned.1.call-update) | async-done | bytes 7526416 | tf_op jit(solution)/shard_map/all_gather | solution.py:101
  237.6 16.6 reshape.818
  274.7 15.2 all-to-all-done.2
  315.8 19.5 all-to-all-done
  405.4 21.6 reshape.825
  427.0 12.8 multiply_convert_fusion.4
  439.7 12.4 multiply_convert_fusion.5
  452.1 21.2 reshape.826
  473.4 12.3 convert_reduce_fusion
  485.6 9.0 fusion.184
  494.7 11.0 convert_reduce_fusion.1
  505.8 10.4 multiply_reduce_fusion.5
  535.1 12.3 all-to-all-done.6
  614.3 9.2 multiply_reduce_fusion.1
  668.8 13.7 all-to-all-done.5
  727.2 34.9 %all-to-all-done.8 = bf16[256,4,1120]{0,2,1:T(8,128)(2,1)} async-done(((bf16[256,4,1120]{0,2,1:T(8,128)(2,1)}), bf16[256,4,1120]{0,2,1:T(8,128)(2,1)}, u32[]{:S(2)}, u32[]{:S(2)}) %all-to-all-start.8) | async-done | bytes 2293792 | tf_op jit(solution)/shard_map/all_to_all | solution.py:229
  778.5 15.7 copy.207
  811.1 9.6 convolution_add_fusion.1
  848.2 23.6 %all-to-all-done.10 = bf16[256,4,1120]{0,2,1:T(8,128)(2,1)} async-done(((bf16[256,4,1120]{0,2,1:T(8,128)(2,1)}), bf16[256,4,1120]{0,2,1:T(8,128)(2,1)}, u32[]{:S(2)}, u32[]{:S(2)}) %all-to-all-start.10) | async-done | bytes 2293792 | tf_op jit(solution)/shard_map/all_to_all | solution.py:222
  880.9 23.3 %all-to-all-done.11 = bf16[256,4,1120]{0,2,1:T(8,128)(2,1)} async-done(((bf16[256,4,1120]{0,2,1:T(8,128)(2,1)}), bf16[256,4,1120]{0,2,1:T(8,128)(2,1)}, u32[]{:S(2)}, u32[]{:S(2)}) %all-to-all-start.11) | async-done | bytes 2293792 | tf_op jit(solution)/shard_map/all_to_all | solution.py:222
  916.5 9.6 convolution_add_fusion
  959.6 16.2 copy.205
  976.7 9.2 fusion.46
  999.2 46.6 %all-reduce.4 = (f32[1120]{0:T(1024)}, f32[1120]{0:T(1024)}, f32[2240]{0:T(1024)}, f32[1120]{0:T(1024)}, f32[1120]{0:T(1024)}, /*index=5*/f32[1120]{0:T(1024)}, f32[4480]{0:T(1024)}, f32[1120]{0:T(1024)}) all-reduce(f32[1120]{0:T(1024)S(1)} %add.414, f32[1120]{0:T(1024)S(1)} %add.415, ...), channel_id=1, replica_groups=mesh['wide'=8,'narrow'=4] {'wide','narrow'}, use_global_device_ids=true, to_apply=%region_34.35 | all-reduce | flops 13440 | bytes 107520 | tf_op jit(solution)/shard_map/psum | solution.py:302
  1050.6 262.8 %reduce-scatter.15.cloned.1.call-done = f32[7840,5]{1,0:T(8,128)} async-done(((f32[62720,5]{1,0:T(8,128)}), f32[7840,5]{1,0:T(8,128)}) %reduce-scatter.15.cloned.1.call-update) | async-done | bytes 156816
  1316.9 159.5 %reduce-scatter.17.cloned.1.call-done = f32[1120,140]{1,0:T(8,128)} async-done(((f32[8960,140]{1,0:T(8,128)}), f32[1120,140]{1,0:T(8,128)}) %reduce-scatter.17.cloned.1.call-update) | async-done | bytes 627216
  1478.8 160.0 %reduce-scatter.19.cloned.1.call-done = f32[1120,140]{1,0:T(8,128)} async-done(((f32[8960,140]{1,0:T(8,128)}), f32[1120,140]{1,0:T(8,128)}) %reduce-scatter.19.cloned.1.call-update) | async-done | bytes 627216
  1641.2 516.8 %reduce-scatter.13.cloned.1.call-done = f32[7840,15]{1,0:T(8,128)} async-done(((f32[62720,15]{1,0:T(8,128)}), f32[7840,15]{1,0:T(8,128)}) %reduce-scatter.13.cloned.1.call-update) | async-done | bytes 470416
  (459 shorter events, 468.8 us)
Async XLA Ops:
  7.2 54.3 %all-gather.42.cloned.1.call-start = ((), (), s32[]{:S(2)}) async-start(), calls=%async_computation.24 | async-start | bytes 2285568 | tf_op jit(solution)/shard_map/all_gather | solution.py:95
  7.9 117.0 %all-gather.48.cloned.1.call-start = ((), (), s32[]{:S(2)}) async-start(), calls=%async_computation.27 | async-start | bytes 2985984 | tf_op jit(solution)/shard_map/all_gather | solution.py:97
  8.7 172.6 %all-gather.52.cloned.1.call-start = ((), (), s32[]{:S(2)}) async-start(), calls=%async_computation.29 | async-start | bytes 2985984 | tf_op jit(solution)/shard_map/all_gather | solution.py:98
  9.4 228.2 %all-gather.44.cloned.1.call-start = ((), (), s32[]{:S(2)}) async-start(), calls=%async_computation.25 | async-start | bytes 10035200 | tf_op jit(solution)/shard_map/all_gather | solution.py:101
  67.8 302.5 %all-gather.46.cloned.1.call-start = ((), (), s32[]{:S(2)}) async-start(), calls=%async_computation.26 | async-start | bytes 5017600 | tf_op jit(solution)/shard_map/all_gather | solution.py:102
  104.2 301.3 %all-gather.50.cloned.1.call-start = ((), (), s32[]{:S(2)}) async-start(), calls=%async_computation.28 | async-start | bytes 12902400 | tf_op jit(solution)/shard_map/all_gather | solution.py:103
  131.3 320.8 %all-gather.54.cloned.1.call-start = ((), (), s32[]{:S(2)}) async-start(), calls=%async_computation.30 | async-start | bytes 12902400 | tf_op jit(solution)/shard_map/all_gather | solution.py:104
  135.3 132.4 %copy-start.56 = (f32[256]{0:T(256)}, f32[256]{0:T(256)S(1)}, u32[]{:S(2)}) copy-start(f32[256]{0:T(256)S(1)} %get-tuple-element.302) | copy-start | bytes 3076
  261.2 28.7 %all-to-all-start.2 = ((bf16[256,4,840]{0,2,1:T(8,128)(2,1)}), bf16[256,4,840]{0,2,1:T(8,128)(2,1)S(1)}, u32[]{:S(2)}, u32[]{:S(2)}) async-start(bf16[256,4,840]{0,2,1:T(8,128)(2,1)} %bitcast.490), calls=%async_computation.2 | async-start | bytes 3440640 | tf_op jit(solution)/shard_map/all_to_all | solution.py:172
  289.9 45.3 %all-to-all-start = ((bf16[256,4,840]{0,2,1:T(8,128)(2,1)}), bf16[256,4,840]{0,2,1:T(8,128)(2,1)}, u32[]{:S(2)}, u32[]{:S(2)}) async-start(bf16[256,4,840]{0,2,1:T(8,128)(2,1)} %bitcast.489), calls=%async_computation | async-start | bytes 3440640 | tf_op jit(solution)/shard_map/all_to_all | solution.py:172
  335.2 30.8 %all-to-all-start.3 = ((bf16[4,2,35840]{2,1,0:T(2,128)(2,1)}), bf16[4,2,35840]{2,1,0:T(2,128)(2,1)}, u32[]{:S(2)}, u32[]{:S(2)}) async-start(bf16[4,2,35840]{2,1,0:T(2,128)(2,1)} %reshape.883), calls=%async_computation.3 | async-start | bytes 1146880 | tf_op jit(solution)/shard_map/all_to_all | solution.py:185
  366.1 22.9 %all-to-all-start.1 = ((bf16[4,2,35840]{2,1,0:T(2,128)(2,1)}), bf16[4,2,35840]{2,1,0:T(2,128)(2,1)}, u32[]{:S(2)}, u32[]{:S(2)}) async-start(bf16[4,2,35840]{2,1,0:T(2,128)(2,1)} %reshape.885), calls=%async_computation.1 | async-start | bytes 1146880 | tf_op jit(solution)/shard_map/all_to_all | solution.py:185
  370.2 396.8 %all-gather.30.cloned.1.call-start = ((), (), s32[]{:S(2)}) async-start(), calls=%async_computation.18 | async-start | bytes 2867200 | tf_op jit(solution)/shard_map/all_gather | solution.py:249
  520.5 250.5 %all-gather.32.cloned.1.call-start = ((), (), s32[]{:S(2)}) async-start(), calls=%async_computation.19 | async-start | bytes 2867200 | tf_op jit(solution)/shard_map/all_gather | solution.py:249
  521.2 281.6 %all-gather.34.cloned.1.call-start = ((), (), s32[]{:S(2)}) async-start(), calls=%async_computation.20 | async-start | bytes 2867200 | tf_op jit(solution)/shard_map/all_gather | solution.py:214
  521.8 289.2 %all-gather.36.cloned.1.call-start = ((), (), s32[]{:S(2)}) async-start(), calls=%async_computation.21 | async-start | bytes 2867200 | tf_op jit(solution)/shard_map/all_gather | solution.py:214
  522.6 386.0 %all-gather.38.cloned.1.call-start = ((), (), s32[]{:S(2)}) async-start(), calls=%async_computation.22 | async-start | bytes 2867200 | tf_op jit(solution)/shard_map/all_gather | solution.py:215
  528.1 19.3 all-to-all-start.6
  547.4 17.1 all-to-all-start.4
  609.2 40.3 %all-to-all-start.7 = ((bf16[4,2,107520]{2,1,0:T(2,128)(2,1)}), bf16[4,2,107520]{2,1,0:T(2,128)(2,1)}, u32[]{:S(2)}, u32[]{:S(2)}) async-start(bf16[4,2,107520]{2,1,0:T(2,128)(2,1)} %reshape.889), calls=%async_computation.7 | async-start | bytes 3440640 | tf_op jit(solution)/shard_map/all_to_all | solution.py:275
  649.5 33.1 %all-to-all-start.5 = ((bf16[4,2,107520]{2,1,0:T(2,128)(2,1)}), bf16[4,2,107520]{2,1,0:T(2,128)(2,1)}, u32[]{:S(2)}, u32[]{:S(2)}) async-start(bf16[4,2,107520]{2,1,0:T(2,128)(2,1)} %reshape.887), calls=%async_computation.5 | async-start | bytes 3440640 | tf_op jit(solution)/shard_map/all_to_all | solution.py:275
  653.9 262.6 %all-gather.40.cloned.1.call-start = ((), (), s32[]{:S(2)}) async-start(), calls=%async_computation.23 | async-start | bytes 2867200 | tf_op jit(solution)/shard_map/all_gather | solution.py:215
  654.7 286.5 %all-gather.26.cloned.1.call-start = ((), (), s32[]{:S(2)}) async-start(), calls=%async_computation.16 | async-start | bytes 2867200 | tf_op jit(solution)/shard_map/all_gather | solution.py:213
  713.6 233.9 %all-gather.28.cloned.1.call-start = ((), (), s32[]{:S(2)}) async-start(), calls=%async_computation.17 | async-start | bytes 2867200 | tf_op jit(solution)/shard_map/all_gather | solution.py:213
  718.4 43.7 %all-to-all-start.8 = ((bf16[256,4,1120]{0,2,1:T(8,128)(2,1)}), bf16[256,4,1120]{0,2,1:T(8,128)(2,1)}, u32[]{:S(2)}, u32[]{:S(2)}) async-start(bf16[256,4,1120]{0,2,1:T(8,128)(2,1)} %bitcast.465), calls=%async_computation.8 | async-start | bytes 4587520 | tf_op jit(solution)/shard_map/all_to_all | solution.py:229
  762.1 36.5 %all-to-all-start.9 = ((bf16[256,4,1120]{0,2,1:T(8,128)(2,1)}), bf16[256,4,1120]{0,2,1:T(8,128)(2,1)}, u32[]{:S(2)}, u32[]{:S(2)}) async-start(bf16[256,4,1120]{0,2,1:T(8,128)(2,1)} %bitcast.463), calls=%async_computation.9 | async-start | bytes 4587520 | tf_op jit(solution)/shard_map/all_to_all | solution.py:229
  767.0 546.4 %reduce-scatter.15.cloned.1.call-start = ((), (), s32[]{:S(2)}) async-start(), calls=%async_computation.32 | async-start | bytes 36126720
  794.2 682.2 %reduce-scatter.17.cloned.1.call-start = ((), (), s32[]{:S(2)}) async-start(), calls=%async_computation.33 | async-start | bytes 10321920
  839.5 32.3 %all-to-all-start.10 = ((bf16[256,4,1120]{0,2,1:T(8,128)(2,1)}), bf16[256,4,1120]{0,2,1:T(8,128)(2,1)}, u32[]{:S(2)}, u32[]{:S(2)}) async-start(bf16[256,4,1120]{0,2,1:T(8,128)(2,1)} %bitcast.466), calls=%async_computation.10 | async-start | bytes 4587520 | tf_op jit(solution)/shard_map/all_to_all | solution.py:222
  871.8 32.4 %all-to-all-start.11 = ((bf16[256,4,1120]{0,2,1:T(8,128)(2,1)}), bf16[256,4,1120]{0,2,1:T(8,128)(2,1)}, u32[]{:S(2)}, u32[]{:S(2)}) async-start(bf16[256,4,1120]{0,2,1:T(8,128)(2,1)} %bitcast.464), calls=%async_computation.11 | async-start | bytes 4587520 | tf_op jit(solution)/shard_map/all_to_all | solution.py:222
  876.4 762.4 %reduce-scatter.19.cloned.1.call-start = ((), (), s32[]{:S(2)}) async-start(), calls=%async_computation.34 | async-start | bytes 10321920
  941.0 1217.0 %reduce-scatter.13.cloned.1.call-start = ((), (), s32[]{:S(2)}) async-start(), calls=%async_computation.31 | async-start | bytes 36126720
  (99 other events, 1291.0 us)
Sparse Core Ops, SparseCore 0:
  10.2 51.2 all-gather.41
  63.7 61.2 all-gather.47
  127.1 54.1 all-gather.51
  182.7 54.8 all-gather.43
  239.6 37.0 all-gather.45
  278.0 94.1 all-gather.49
  373.8 69.2 all-gather.53
  520.6 31.5 all-gather.29
  554.3 23.9 all-gather.31
  579.7 23.9 all-gather.33
  605.3 34.6 all-gather.35
  641.4 31.3 all-gather.37
  674.3 24.3 all-gather.39
  713.7 34.0 all-gather.25
  749.2 28.0 all-gather.27
  794.3 519.0 reduce-scatter.14
  1317.4 158.8 reduce-scatter.16
  1479.9 158.8 reduce-scatter.18
  1642.9 515.1 reduce-scatter.12
where the time goes:
time: 2180 us; the launch traced here: 2170 us
  waiting for transfers between devices  1410 us (65%)
  local copies, waits for them, and re-layouts  308 us (14%)
  matrix products  246 us (11%)
  blocking collectives  80.8 us (4%)
  starting transfers between devices  53.6 us (2%)
  other arithmetic  51.9 us (2%)
    unnamed x23, waiting for transfers between devices  1100 us
    unnamed x226, local copies, waits for them, and re-layouts  134 us
    all_gather x1, waiting for transfers between devices, gather_batch(): lax.all_gather(shards[0], 'wide', axis=1, tiled=True)  52 us
    all_to_all x2, waiting for transfers between devices, on_device(): lax.all_to_all(hidden_low.reshape(local_rows, groups, ff_here), 'narrow',...  46.9 us
    all_gather x1, waiting for transfers between devices, gather_batch(): lax.all_gather(columns[0], 'narrow', axis=0, tiled=True)  46.9 us
    psum x1, blocking collectives, on_device(): small_totals = lax.psum(small_store, ('wide', 'narrow'))  46.6 us
    all_gather x1, waiting for transfers between devices, gather_batch(): lax.all_gather(shards[3], 'wide', axis=1, tiled=True)  44.7 us
  transfers between devices with their start and end apart: 31, of which 15 were waited for; matrix products, arithmetic and copies ran while one was open for 24% of the time, Pallas kernels for 0%

commit v1 on v0

v1 whole, which is shorter than its diff:
```python
import functools

import jax
import jax.numpy as jnp
from jax import lax
from jax.experimental import pallas as pl
from jax.experimental.pallas import tpu as pltpu
from jax.sharding import PartitionSpec as P

HEAD_DIM = 56
PAD_DIM = 64
OUTER = 8
NORM_EPS = 1e-05
MESH = pl.DeviceIdType.MESH
BF16 = jnp.bfloat16
F32 = jnp.float32
PIECE = 48
SCALE = HEAD_DIM ** (-0.5)


def place(inner):
    w = lax.axis_index("wide")
    n = lax.axis_index("narrow")
    outer = w // inner
    return outer // 2, outer % 2, n // 2, n % 2, w % inner


def device(inner, z, x, y, c, wi):
    return ((2 * z + x) * inner + wi, 2 * y + c)


def slab(y, x, z):
    return y * 8 + x * 4 + z


def remote(src, dst, send, recv, dev):
    return pltpu.make_async_remote_copy(
        src_ref=src, dst_ref=dst, send_sem=send, recv_sem=recv, device_id=dev, device_id_type=MESH
    )


def greet(devices):
    barrier = pltpu.get_barrier_semaphore()
    for dev in devices:
        pl.semaphore_signal(barrier, inc=1, device_id=dev, device_id_type=MESH)
    pl.semaphore_wait(barrier, len(devices))


def neighbours(inner):
    z, x, y, c, wi = place(inner)
    along = [device(inner, (z + d) % 4, x, y, c, wi) for d in (1, 2, 3)]
    return (
        along,
        device(inner, z, 1 - x, y, c, wi),
        device(inner, z, x, 1 - y, c, wi),
        device(inner, z, x, y, 1 - c, wi),
    )


def gather_kernel(inner, blocks, pieces, *refs):
    w_refs, x_ref, g_ref = refs[:blocks], refs[blocks], refs[blocks + 1]
    outs = refs[blocks + 2 : 2 * blocks + 2]
    xo, go = refs[2 * blocks + 2], refs[2 * blocks + 3]
    zs, zr, xs, xr, ys, yr, fxs, fxr, fys, fyr, ss, sr, ls = refs[2 * blocks + 4 :]
    z, x, y, c, wi = place(inner)
    along, xdev, ydev, cdev = neighbours(inner)
    greet([*along, xdev, ydev, cdev])

    total = blocks * pieces

    def view(k, s):
        b, p = k // pieces, k % pieces
        return outs[b].at[s, pl.ds(p * PIECE, PIECE)]

    def own(k):
        b, p = k // pieces, k % pieces
        return w_refs[b].at[pl.ds(p * PIECE, PIECE)]

    locals_ = [
        pltpu.make_async_copy(w_refs[b], outs[b].at[slab(y, x, z)], ls.at[b]) for b in range(blocks)
    ]

    def zcopy(k, d):
        return remote(own(k), view(k, slab(y, x, z)), zs.at[k, d - 1], zr.at[k, d - 1], along[d - 1])

    def zwait(k, d):
        v = view(k, slab(y, x, (z + 4 - d) % 4))
        return remote(v, v, zs.at[k, d - 1], zr.at[k, d - 1], along[d - 1])

    def xcopy(k, d):
        s = slab(y, x, (z + 4 - d) % 4)
        src = own(k) if d == 0 else view(k, s)
        return remote(src, view(k, s), xs.at[k, d], xr.at[k, d], xdev)

    def xwait(k, d):
        v = view(k, slab(y, 1 - x, (z + 4 - d) % 4))
        return remote(v, v, xs.at[k, d], xr.at[k, d], xdev)

    def ycopy(k, d):
        s = slab(y, x, (z + 4 - d) % 4)
        src = own(k) if d == 0 else view(k, s)
        return remote(src, view(k, s), ys.at[k, d], yr.at[k, d], ydev)

    def ywait(k, d):
        v = view(k, slab(1 - y, x, (z + 4 - d) % 4))
        return remote(v, v, ys.at[k, d], yr.at[k, d], ydev)

    def fycopy(k, d):
        v = view(k, slab(y, 1 - x, (z + 4 - d) % 4))
        return remote(v, v, fys.at[k, d], fyr.at[k, d], ydev)

    def fywait(k, d):
        v = view(k, slab(1 - y, 1 - x, (z + 4 - d) % 4))
        return remote(v, v, fys.at[k, d], fyr.at[k, d], ydev)

    def fxcopy(k, d):
        v = view(k, slab(1 - y, x, (z + 4 - d) % 4))
        return remote(v, v, fxs.at[k, d - 2], fxr.at[k, d - 2], xdev)

    def fxwait(k, d):
        v = view(k, slab(1 - y, 1 - x, (z + 4 - d) % 4))
        return remote(v, v, fxs.at[k, d - 2], fxr.at[k, d - 2], xdev)

    def a1(k):
        for d in (1, 2, 3):
            zcopy(k, d).start()
        xcopy(k, 0).start()
        ycopy(k, 0).start()

    def a2(k):
        for d in (1, 2, 3):
            zwait(k, d).wait_recv()
            xcopy(k, d).start()
            ycopy(k, d).start()

    def a3(k):
        for d in (0, 1):
            xwait(k, d).wait_recv()
            fycopy(k, d).start()
            ywait(k, d + 2).wait_recv()
            fxcopy(k, d + 2).start()

    def a4(k):
        for d in (0, 1):
            xwait(k, d + 2).wait_recv()
            ywait(k, d).wait_recv()
            fywait(k, d).wait_recv()
            fxwait(k, d + 2).wait_recv()

    n_own = 2 * y + c
    n_sib = 2 * y + 1 - c
    n_y = 2 * (1 - y) + c
    n_ys = 2 * (1 - y) + 1 - c

    def swap(i, src, dst):
        mine = pltpu.make_async_copy(src.at[y], dst.at[n_own], ls.at[blocks + i])
        side = remote(src.at[y], dst.at[n_own], ss.at[i, 0], sr.at[i, 0], cdev)
        over = remote(src.at[1 - y], dst.at[n_own], ss.at[i, 1], sr.at[i, 1], ydev)
        over_in = remote(dst.at[n_y], dst.at[n_y], ss.at[i, 1], sr.at[i, 1], ydev)
        fwd = remote(dst.at[n_y], dst.at[n_y], ss.at[i, 2], sr.at[i, 2], cdev)
        return mine, side, over, over_in, fwd

    def swap_start(parts):
        parts[0].start()
        parts[1].start()
        parts[2].start()

    def swap_mid(parts):
        parts[3].wait_recv()
        parts[4].start()

    def swap_end(i, dst, parts):
        parts[0].wait()
        side_in = remote(dst.at[n_sib], dst.at[n_sib], ss.at[i, 0], sr.at[i, 0], cdev)
        fwd_in = remote(dst.at[n_ys], dst.at[n_ys], ss.at[i, 2], sr.at[i, 2], cdev)
        side_in.wait_recv()
        fwd_in.wait_recv()
        parts[1].wait_send()
        parts[2].wait_send()
        parts[4].wait_send()

    xp = swap(0, x_ref, xo)
    gp = swap(1, g_ref, go)
    swap_start(xp)
    a1(0)
    for b in range(blocks):
        locals_[b].start()
    for k in range(total + 2):
        if k + 1 < total:
            a1(k + 1)
        if k < total:
            a2(k)
        if 0 <= k - 1 < total:
            a3(k - 1)
        if 0 <= k - 2 < total:
            a4(k - 2)
        if k == 0:
            swap_mid(xp)
        if k == 3:
            swap_start(gp)
        if k == 6:
            swap_mid(gp)
    swap_end(0, xo, xp)
    swap_end(1, go, gp)
    for b in range(blocks):
        locals_[b].wait()
    for k in range(total):
        for d in (1, 2, 3):
            zcopy(k, d).wait_send()
        for d in range(4):
            xcopy(k, d).wait_send()
            ycopy(k, d).wait_send()
        for d in (0, 1):
            fycopy(k, d).wait_send()
            fxcopy(k, d + 2).wait_send()


def gather_all(inner, weights, cells, cot):
    blocks = len(weights)
    rows, width = weights[0].shape
    pieces = rows // PIECE
    total = blocks * pieces
    dma = pltpu.SemaphoreType.DMA
    any_ = pl.BlockSpec(memory_space=pl.ANY)
    local_rows = cells.shape[1]
    return pl.pallas_call(
        functools.partial(gather_kernel, inner, blocks, pieces),
        out_shape=[jax.ShapeDtypeStruct((16, rows, width), BF16)] * blocks
        + [jax.ShapeDtypeStruct((4, local_rows, width), BF16)] * 2,
        in_specs=[any_] * (blocks + 2),
        out_specs=[any_] * (blocks + 2),
        scratch_shapes=[
            dma((total, 3)), dma((total, 3)),
            dma((total, 4)), dma((total, 4)),
            dma((total, 4)), dma((total, 4)),
            dma((total, 2)), dma((total, 2)),
            dma((total, 2)), dma((total, 2)),
            dma((2, 3)), dma((2, 3)),
            dma((blocks + 2,)),
        ],
        compiler_params=pltpu.CompilerParams(collective_id=0, has_side_effects=True),
        name="gather_weights",
    )(*weights, cells, cot)


def reduce_kernel(inner, blocks, pieces, *refs):
    parts, small = refs[:blocks], refs[blocks]
    out, small_out = refs[blocks + 1], refs[blocks + 2]
    r1, rx, ry, rz, sx, sy, st, own32 = refs[blocks + 3 : blocks + 11]
    acc, got = refs[blocks + 11 : blocks + 13]
    s1, q1, s2, q2, s3, q3, sz, qz, sa, qa = refs[blocks + 13 :]
    z, x, y, c, wi = place(inner)
    along, xdev, ydev, cdev = neighbours(inner)
    greet([*along, xdev, ydev, cdev])
    total = blocks * pieces

    def rows(k):
        return parts[k // pieces], pl.ds((k % pieces) * PIECE, PIECE)

    def cut(k, s, count):
        ref, r = rows(k)
        return ref.at[pl.ds(s, count), r]

    def load(k, s, count):
        ref, r = rows(k)
        return ref[pl.ds(s, count), r].astype(F32)

    def first(k):
        return (
            remote(cut(k, slab(1 - y, 1 - x, 0), 2), r1.at[k, pl.ds(0, 2)], s1.at[k, 0], q1.at[k, 0], ydev),
            remote(cut(k, slab(1 - y, 1 - x, 2), 2), r1.at[k, pl.ds(2, 2)], s1.at[k, 1], q1.at[k, 1], xdev),
        )

    def second(k):
        return (
            remote(cut(k, slab(y, 1 - x, 2), 2), rx.at[k, pl.ds(2, 2)], s2.at[k, 0], q2.at[k, 0], xdev),
            remote(cut(k, slab(1 - y, x, 0), 2), ry.at[k, pl.ds(0, 2)], s2.at[k, 1], q2.at[k, 1], ydev),
        )

    def third(k):
        return (
            remote(sx.at[k], rx.at[k, pl.ds(0, 2)], s3.at[k, 0], q3.at[k, 0], xdev),
            remote(sy.at[k], ry.at[k, pl.ds(2, 2)], s3.at[k, 1], q3.at[k, 1], ydev),
        )

    def last(k, d):
        return remote(st.at[k, d - 1], rz.at[k, d - 1], sz.at[k, d - 1], qz.at[k, d - 1], along[d - 1])

    def stage1(k):
        for cp in (*first(k), *second(k)):
            cp.start()

    def stage2(k):
        f = first(k)
        t = third(k)
        f[0].wait_recv()
        sx[k] = (load(k, slab(y, 1 - x, 0), 2) + r1[k, 0:2].astype(F32)).astype(BF16)
        t[0].start()
        f[1].wait_recv()
        sy[k] = (load(k, slab(1 - y, x, 2), 2) + r1[k, 2:4].astype(F32)).astype(BF16)
        t[1].start()

    def stage3(k):
        for cp in (*second(k), *third(k)):
            cp.wait_recv()
        for d in (1, 2, 3):
            j = (z + d) % 4
            st[k, d - 1] = (
                load(k, slab(y, x, j), 1)[0] + rx[k, j].astype(F32) + ry[k, j].astype(F32)
            ).astype(BF16)
            last(k, d).start()
        own32[k] = load(k, slab(y, x, z), 1)[0] + rx[k, z].astype(F32) + ry[k, z].astype(F32)

    def stage4(k):
        for d in (1, 2, 3):
            last(k, d).wait_recv()
        out[k] = (
            own32[k] + rz[k, 0].astype(F32) + rz[k, 1].astype(F32) + rz[k, 2].astype(F32)
        )

    peers = [
        cdev, xdev, ydev,
        device(inner, z + 1 - 2 * (z % 2), x, y, c, wi),
        device(inner, (z + 2) % 4, x, y, c, wi),
    ]

    def small_copy(i):
        return remote(acc.at[i], got.at[i], sa.at[i], qa.at[i], peers[i])

    acc[0] = small[...]
    for k in range(total + 2):
        if k < total:
            stage1(k)
        if k < 5:
            small_copy(k).start()
        if k < total:
            stage2(k)
        if 0 <= k - 1 < total:
            stage3(k - 1)
        if 0 <= k - 2 < total:
            stage4(k - 2)
        if k < 5:
            small_copy(k).wait()
            acc[k + 1] = acc[k] + got[k]
    small_out[...] = acc[5]
    for k in range(total):
        for cp in (*first(k), *second(k), *third(k), last(k, 1), last(k, 2), last(k, 3)):
            cp.wait_send()


def reduce_all(inner, parts, small):
    blocks = len(parts)
    rows, width = parts[0].shape[1:]
    pieces = rows // PIECE
    total = blocks * pieces
    dma = pltpu.SemaphoreType.DMA
    vm = pl.BlockSpec(memory_space=pltpu.VMEM)
    out, small_sum = pl.pallas_call(
        functools.partial(reduce_kernel, inner, blocks, pieces),
        out_shape=[
            jax.ShapeDtypeStruct((total, PIECE, width), F32),
            jax.ShapeDtypeStruct(small.shape, F32),
        ],
        in_specs=[vm] * (blocks + 1),
        out_specs=[vm, vm],
        scratch_shapes=[
            pltpu.VMEM((total, 4, PIECE, width), BF16),
            pltpu.VMEM((total, 4, PIECE, width), BF16),
            pltpu.VMEM((total, 4, PIECE, width), BF16),
            pltpu.VMEM((total, 3, PIECE, width), BF16),
            pltpu.VMEM((total, 2, PIECE, width), BF16),
            pltpu.VMEM((total, 2, PIECE, width), BF16),
            pltpu.VMEM((total, 3, PIECE, width), BF16),
            pltpu.VMEM((total, PIECE, width), F32),
            pltpu.VMEM((6, *small.shape), F32),
            pltpu.VMEM((5, *small.shape), F32),
            dma((total, 2)), dma((total, 2)),
            dma((total, 2)), dma((total, 2)),
            dma((total, 2)), dma((total, 2)),
            dma((total, 3)), dma((total, 3)),
            dma((5,)), dma((5,)),
        ],
        compiler_params=pltpu.CompilerParams(
            collective_id=1, has_side_effects=True, vmem_limit_bytes=62 * 2**20
        ),
        name="reduce_grads",
    )(*parts, small)
    return out.reshape(blocks, rows, width), small_sum


def dot(a, b, dims):
    return lax.dot_general(a, b, (dims, ((), ())), preferred_element_type=F32)


def dot_nn(a, b):
    return dot(a, b, ((1,), (0,)))


def dot_nt(a, b):
    return dot(a, b, ((1,), (1,)))


def dot_tn(a, b):
    return dot(a, b, ((0,), (0,)))


def norm_parts(v):
    center = v - jnp.mean(v, axis=-1, keepdims=True)
    rstd = lax.rsqrt(jnp.mean(center * center, axis=-1, keepdims=True) + NORM_EPS)
    return center * rstd, rstd


def norm_back(e, gain, xhat, rstd):
    eg = e * gain
    return rstd * (
        eg - jnp.mean(eg, axis=-1, keepdims=True) - xhat * jnp.mean(eg * xhat, axis=-1, keepdims=True)
    )


def attend(q, k, v, cell_len):
    heads, total = q.shape[0], q.shape[1]
    block = min(512, total)
    outs, sums = [], []
    for start in range(0, total, block):
        end = start + block
        allowed = visible(start, block, end, cell_len)
        s = jnp.einsum("hqe,hke->hqk", q[:, start:end], k[:, :end], preferred_element_type=F32) * SCALE
        s = jnp.where(allowed[None], s, -1e30)
        m = jnp.max(s, axis=-1, keepdims=True)
        e = jnp.exp(s - m)
        t = jnp.sum(e, axis=-1, keepdims=True)
        p = (e / t).astype(BF16)
        outs.append(jnp.einsum("hqk,hke->hqe", p, v[:, :end], preferred_element_type=F32).astype(BF16))
        sums.append(m + jnp.log(t))
    return jnp.concatenate(outs, axis=1), sums


def visible(start, rows, count, cell_len):
    qp = start + jnp.arange(rows, dtype=jnp.int32)[:, None]
    kp = jnp.arange(count, dtype=jnp.int32)[None, :]
    return (kp <= qp) & (kp < cell_len)


def attend_back(q, k, v, g, cell_len, sums):
    total = q.shape[1]
    block = min(512, total)
    gq = []
    gk = jnp.zeros(k.shape, F32)
    gv = jnp.zeros(v.shape, F32)
    for i, start in enumerate(range(0, total, block)):
        end = start + block
        allowed = visible(start, block, end, cell_len)
        qb, gb = q[:, start:end], g[:, start:end]
        s = jnp.einsum("hqe,hke->hqk", qb, k[:, :end], preferred_element_type=F32) * SCALE
        s = jnp.where(allowed[None], s, -1e30)
        p = jnp.exp(s - sums[i])
        pl_ = p.astype(BF16)
        gv = gv.at[:, :end].add(jnp.einsum("hqk,hqe->hke", pl_, gb, preferred_element_type=F32))
        gp = jnp.einsum("hqe,hke->hqk", gb, v[:, :end], preferred_element_type=F32)
        inner = jnp.sum(p * gp, axis=-1, keepdims=True)
        gs = (p * (gp - inner)).astype(BF16)
        gq.append(jnp.einsum("hqk,hke->hqe", gs, k[:, :end], preferred_element_type=F32) * SCALE)
        gk = gk.at[:, :end].add(jnp.einsum("hqk,hqe->hke", gs, qb, preferred_element_type=F32) * SCALE)
    return jnp.concatenate(gq, axis=1), gk, gv


def order_matrix():
    heads = 5
    dst = jnp.arange(4 * heads * PAD_DIM, dtype=jnp.int32)[:, None]
    src = jnp.arange(OUTER * 144, dtype=jnp.int32)[None, :]
    xz, i = src // 144, src % 144
    w = 2 * (xz % 4) + xz // 4
    e = i % 7
    group = i // 7
    part = jnp.where(group < 15, group % 3, 3)
    head = jnp.where(group < 15, group // 3, group - 15)
    want = part * heads * PAD_DIM + head * PAD_DIM + w * 7 + e
    return ((dst == want) & (i < 140)).astype(BF16)


def gelu(u):
    t = jnp.tanh(0.7978845608 * (u + 0.044715 * u * u * u))
    h = 0.5 * u * (1.0 + t)
    d = 0.5 * (1.0 + t) + 0.5 * u * (1.0 - t * t) * 0.7978845608 * (1.0 + 3 * 0.044715 * u * u)
    return h, d


def pad_rows(a, rows):
    return jnp.pad(a, ((0, rows - a.shape[0]), (0, 0)))


def on_device(
    cells_in, lengths, w_qkv, w_out, w_up, w_down, ln1_gain, ln1_shift, bias_qv, bias_out,
    ln2_gain, ln2_shift, bias_up, bias_down, cotangent,
):
    wide = lax.axis_size("wide")
    inner = wide // OUTER
    shards = [w_qkv, w_out, w_up, w_down]
    if inner > 1:
        groups = [[o * inner + i for i in range(inner)] for o in range(OUTER)]
        shards = [
            lax.all_gather(s, "wide", axis=1, tiled=True, axis_index_groups=groups) for s in shards
        ]
    width = cells_in.shape[3]
    local_rows = cells_in.shape[2]
    heads = width // HEAD_DIM // 2
    n = lax.axis_index("narrow")
    y, c = n // 2, n % 2
    w_a = jnp.concatenate([shards[0].reshape(-1, width), shards[1].reshape(-1, width)], axis=0)
    rows = -(-w_a.shape[0] // PIECE) * PIECE
    w_a = pad_rows(w_a, rows)
    w_u = pad_rows(shards[2].reshape(-1, width), rows)
    w_d = pad_rows(shards[3].reshape(-1, width), rows)
    used = shards[2].size // width

    g_a, g_u, g_d, cells, cot = gather_all(inner, (w_a, w_u, w_d), cells_in[:, 0], cotangent[:, 0])
    order = order_matrix()
    mats = [dot_nn(order, g_a.reshape(2, OUTER * rows, width)[i]).astype(BF16) for i in range(2)]
    half = heads // 2 * PAD_DIM
    w_parts = [jnp.concatenate([m[p * half : (p + 1) * half] for m in mats], axis=0) for p in range(4)]
    wq, wk, wv, wo = w_parts
    wu = g_u.reshape(16 * rows, width)
    wd = g_d.reshape(16 * rows, width)

    def pick_heads(b):
        b = b.reshape(2, 2, heads // 2, HEAD_DIM)
        b = lax.dynamic_index_in_dim(b, c, axis=1, keepdims=False)
        return jnp.pad(b, ((0, 0), (0, 0), (0, PAD_DIM - HEAD_DIM))).reshape(-1)

    bq = pick_heads(bias_qv[:width])
    bv = pick_heads(bias_qv[width:])

    b_u = bias_up.reshape(2, 2, used, 4, 2)
    b_u = lax.dynamic_index_in_dim(b_u, c, axis=1, keepdims=False).transpose(0, 3, 2, 1)
    b_u = jnp.pad(b_u, ((0, 0), (0, 0), (0, 0), (0, rows - used))).reshape(-1)

    total = 4 * local_rows
    x32 = cells.reshape(total, width).astype(F32)
    cell_len = lax.dynamic_index_in_dim(lengths[:, 0], y, keepdims=False)
    xhat1, rstd1 = norm_parts(x32)
    normed = (xhat1 * ln1_gain + ln1_shift).astype(BF16)
    q = (dot_nt(normed, wq) + bq).astype(BF16)
    k = dot_nt(normed, wk).astype(BF16)
    v = (dot_nt(normed, wv) + bv).astype(BF16)

    def split(a):
        return a.reshape(total, heads, PAD_DIM).transpose(1, 0, 2)

    def join(a):
        return a.transpose(1, 0, 2).reshape(total, heads * PAD_DIM)

    qh, kh, vh = split(q), split(k), split(v)
    mixed_h, sums = attend(qh, kh, vh, cell_len)
    mixed = join(mixed_h)

    sibling = [(0, 1), (1, 0), (2, 3), (3, 2)]

    def own_rows(a):
        a = a.reshape(2, 2, local_rows, a.shape[-1])
        return lax.dynamic_index_in_dim(a, c, axis=1, keepdims=False).reshape(2 * local_rows, -1)

    def other_rows(a):
        a = a.reshape(2, 2, local_rows, a.shape[-1])
        return lax.dynamic_index_in_dim(a, 1 - c, axis=1, keepdims=False).reshape(2 * local_rows, -1)

    def pair_sum(a):
        got = lax.ppermute(other_rows(a).astype(BF16), "narrow", sibling)
        return own_rows(a) + got.astype(F32)

    def pair_gather(a):
        got = lax.ppermute(a, "narrow", sibling)
        a = a.reshape(2, local_rows, -1)
        got = got.reshape(2, local_rows, -1)
        first = jnp.where(c == 0, a, got)
        second = jnp.where(c == 0, got, a)
        return jnp.stack([first, second], axis=1).reshape(total, -1)

    middle = own_rows(x32) + pair_sum(dot_nn(mixed, wo)) + bias_out
    xhat2, rstd2 = norm_parts(middle)
    normed2 = pair_gather((xhat2 * ln2_gain + ln2_shift).astype(BF16))
    upper = dot_nt(normed2, wu) + b_u
    hidden, slope = gelu(upper)
    hidden = hidden.astype(BF16)
    g_all = cot.reshape(total, width)
    out = (middle + pair_sum(dot_nn(hidden, wd)) + bias_down).astype(BF16)
    grad_upper = (dot_nt(g_all, wd) * slope).astype(BF16)
    p_d = dot_tn(hidden, g_all).astype(BF16).reshape(16, rows, width)
    p_u = dot_tn(grad_upper, normed2).astype(BF16).reshape(16, rows, width)
    gn2 = pair_sum(dot_nn(grad_upper, wu))
    g_own = own_rows(g_all).astype(F32)
    grad_middle = g_own + norm_back(gn2, ln2_gain, xhat2, rstd2)
    grad_att_own = grad_middle.astype(BF16)
    grad_att = pair_gather(grad_att_own)
    grad_mixed = dot_nt(grad_att, wo).astype(BF16)
    gq, gk, gv = attend_back(qh, kh, vh, split(grad_mixed), cell_len, sums)
    gq, gk, gv = (join(a.astype(BF16)) for a in (gq, gk, gv))
    grads_a = [dot_tn(a, normed).astype(BF16) for a in (gq, gk, gv)] + [
        dot_tn(mixed, grad_att).astype(BF16)
    ]
    p_a = []
    for i in range(2):
        stacked = jnp.concatenate([a[i * half : (i + 1) * half] for a in grads_a], axis=0)
        p_a.append(dot_tn(order, stacked).astype(BF16).reshape(OUTER, rows, width))
    p_a = jnp.concatenate(p_a, axis=0)
    gn1 = pair_sum(dot_nn(gq, wq) + dot_nn(gk, wk) + dot_nn(gv, wv))
    xo, ro = own_rows(xhat1), own_rows(rstd1)
    grad_in = (grad_middle + norm_back(gn1, ln1_gain, xo, ro)).astype(BF16)

    def col_sum(a):
        return jnp.sum(a.astype(F32), axis=0)

    def put_heads(s):
        s = s.reshape(2, 1, heads // 2, PAD_DIM)[..., :HEAD_DIM]
        zero = jnp.zeros_like(s)
        return jnp.where(c == 0, jnp.concatenate([s, zero], 1), jnp.concatenate([zero, s], 1)).reshape(-1)

    def put_hidden(s):
        s = s.reshape(2, 2, 4, rows)[..., :used].transpose(0, 3, 2, 1).reshape(2, 1, -1)
        zero = jnp.zeros_like(s)
        return jnp.where(c == 0, jnp.concatenate([s, zero], 1), jnp.concatenate([zero, s], 1)).reshape(-1)

    small = jnp.concatenate(
        [
            col_sum(gn1 * xo), col_sum(gn1),
            put_heads(col_sum(gq)), put_heads(col_sum(gv)),
            col_sum(grad_att_own), col_sum(gn2 * xhat2), col_sum(gn2),
            put_hidden(col_sum(grad_upper)), col_sum(g_own),
        ]
    ).reshape(-1, width)
    small = pad_rows(small, 16)
    reduced, small = reduce_all(inner, (p_d, p_u, p_a), small)

    def swap_back(a):
        a = a.reshape(2, local_rows, width)
        mine = lax.dynamic_index_in_dim(a, y, axis=0, keepdims=False)
        theirs = lax.dynamic_index_in_dim(a, 1 - y, axis=0, keepdims=False)
        got = lax.ppermute(theirs, "narrow", [(0, 2), (1, 3), (2, 0), (3, 1)])
        first = jnp.where(y == 0, mine, got)
        second = jnp.where(y == 0, got, mine)
        return jnp.stack([first, second], axis=0)[:, None]

    out, grad_in = swap_back(out), swap_back(grad_in)
    qkv_rows = shards[0].size // width
    grads = [
        reduced[2][:qkv_rows].reshape(shards[0].shape),
        reduced[2][qkv_rows : qkv_rows + shards[1].size // width].reshape(shards[1].shape),
        reduced[1][:used],
        reduced[0][:used],
    ]
    grads = [g.reshape(s.shape) for g, s in zip(grads, shards)]
    if inner > 1:
        grads = [
            lax.psum_scatter(g, "wide", scatter_dimension=1, axis_index_groups=groups, tiled=True)
            for g in grads
        ]
    hid = bias_up.shape[0] // width
    flat = [
        small[0], small[1], small[2:4].reshape(-1), small[4], small[5], small[6],
        small[7 : 7 + hid].reshape(-1), small[7 + hid],
    ]
    return (out, grad_in, *grads, *flat)


def solution(mesh):
    cell = P(None, "wide", "narrow", None)
    shard = P("narrow", "wide")
    return jax.shard_map(
        on_device,
        mesh=mesh,
        in_specs=(cell, P(None, "wide"), *[shard] * 4, *[P()] * 8, cell),
        out_specs=(cell, cell, *[shard] * 4, *[P()] * 8),
        check_vma=False,
    )
```

time: 2180 us -> 805 us (0.37)
  waiting for transfers between devices: 1410 us -> 5.5 us
  Pallas kernels: 0 us -> 315 us
  local copies, waits for them, and re-layouts: 308 us -> 178 us
  blocking collectives: 80.8 us -> 0 us
  matrix products: 246 us -> 193 us
  starting transfers between devices: 53.6 us -> 3.58 us
  other arithmetic: 51.9 us -> 94.7 us
    unnamed x23 -> x0, waiting for transfers between devices: 1100 us -> none
    pallas_call x0 -> x2, Pallas kernels: none -> 315 us  [the longest x1 163 us: gather_all(): pl.pallas_call(functools.partial(gather_kernel, inner, blocks, pieces), o...]
    all_gather x15 -> x0, waiting for transfers between devices: 165 us -> none  [the longest x1 52 us: gather_batch(): lax.all_gather(shards[0], 'wide', axis=1, tiled=True)]
    all_to_all x12 -> x0, waiting for transfers between devices: 142 us -> none  [the longest x2 46.9 us: on_device(): lax.all_to_all(hidden_low.reshape(local_rows, groups, ff_here), 'narrow',...]
    unnamed x226 -> x166, local copies, waits for them, and re-layouts: 134 us -> 25.6 us
    reshape x10 -> x18, local copies, waits for them, and re-layouts: 73.9 us -> 18.2 us  [the longest x1 7.07 us: own_rows(): a = a.reshape(2, 2, local_rows, a.shape[-1])]
    dot_general x48 -> x34, matrix products: 246 us -> 193 us  [the longest x22 126 us: dot(): return lax.dot_general(a, b, (dims, ((), ())), preferred_element_type=F32)]
    all_to_all x12 -> x0, starting transfers between devices: 52.4 us -> none  [the longest x2 9.46 us: on_device(): lax.all_to_all(grad_upper_low.reshape(local_rows, groups, ff_here), 'narr...]
  transfers between devices with their start and end apart: 31 -> 8, of which waited for: 15 -> 1; matrix products, arithmetic and copies ran while one was open for 24% -> 16% of each run, Pallas kernels for 0% -> 0%
where the time goes in v1:
time: 805 us; the launch traced here: 792 us
  Pallas kernels  315 us (39%)
  matrix products  193 us (24%)
  local copies, waits for them, and re-layouts  178 us (22%)
  other arithmetic  94.7 us (12%)
    pallas_call x1, Pallas kernels, gather_all(): pl.pallas_call(functools.partial(gather_kernel, inner, blocks, pieces), o...  163 us
    pallas_call x1, Pallas kernels, reduce_all(): pl.pallas_call(functools.partial(reduce_kernel, inner, blocks, pieces), o...  152 us
    dot_general x22, matrix products, dot(): return lax.dot_general(a, b, (dims, ((), ())), preferred_element_type=F32)  126 us
    unnamed x166, local copies, waits for them, and re-layouts  25.6 us
    dynamic_slice x9, local copies, waits for them, and re-layouts, own_rows(): lax.dynamic_index_in_dim(a, c, axis=1, keepdims=False)  23.5 us
    convert_element_type x2, other arithmetic, attend_back(): gs = (p * (gp - inner)).astype(BF16)  17.8 us
    reduce_sum x5, other arithmetic, col_sum(): return jnp.sum(a.astype(F32), axis=0)  17.4 us
    reduce_sum x2, other arithmetic, attend(): t = jnp.sum(e, axis=-1, keepdims=True)  17.2 us
  transfers between devices with their start and end apart: 8, of which 1 were waited for; matrix products, arithmetic and copies ran while one was open for 16% of the time, Pallas kernels for 0%

profile of v1, /device:TPU:0, one launch (start us, length us, event | category | flops | bytes accessed | tf_op | source)
XLA Modules:
  0.0 792.1 jit_solution(10769427972824769591)
XLA Ops:
  14.3 163.3 %gather_weights.1 = (bf16[16,144,1120]{2,1,0:T(8,128)(2,1)}, bf16[16,144,1120]{2,1,0:T(8,128)(2,1)}, bf16[16,144,1120]{2,1,0:T(8,128)(2,1)}, bf16[4,256,1120]{2,1,0:T(8,128)(2,1)}, bf16[4,256,1120]{2,1,0:T(8,128)(2,1)}) custom-call(bf16[144,1120]{1,0:T(8,128)(2,1)} %fusion.81.refs_0_, bf16[144,1120]{1,0:T(8,128)(2,1)} %pad.44.refs_1_, ...), custom_call_target="tpu_custom_call" | custom-call | tf_op jit(solution)/shard_map/gather_weights/pallas_call | solution.py:226
  186.3 4.5 convolution_convert_fusion.5
  200.1 6.0 fusion.138
  206.1 5.7 fusion.137
  211.7 12.8 %fusion.13 = f32[10,512]{1,0:T(8,128)S(1)} fusion(f32[10,512,512]{1,2,0:T(8,128)} %get-tuple-element.186, f32[10,512]{1,0:T(8,128)S(1)} %get-tuple-element.185), kind=kLoop, calls=%fused_computation.30 | loop fusion | flops 5237760 | bytes 10526720 | tf_op jit(solution)/shard_map/reduce_sum | solution.py:431
  228.6 6.3 fusion.52
  239.3 9.5 %fusion.55 = bf16[10,512,64]{1,2,0:T(8,128)(2,1)S(1)} fusion(bf16[10,1024,64]{1,2,0:T(8,128)(2,1)} %bitcast.278, f32[10,512,1024]{2,1,0:T(8,128)} %copy-done.2, f32[10,512]{1,0:T(8,128)S(1)} %fusion, f32[10,512]{1,0:T(8,128)S(1)} %get-tuple-element.183), kind=kOutput, calls=%fused_computation.118 | convolution fusion | flops 687144960 | bytes 22978560 | tf_op jit(solution)/shard_map/hqk,hke->hqe/dot_general | solution.py:433
  250.6 4.6 dot_general.119
  306.4 12.0 %multiply_convert_fusion.2 = (bf16[1024,2304]{1,0:T(8,128)(2,1)}, f32[1024,2304]{1,0:T(8,128)}) fusion(f32[2304]{0:T(1024)S(1)} %copy-done.65, bf16[1024,1120]{1,0:T(8,128)(2,1)S(1)} %bitcast.292, bf16[2304,1120]{1,0:T(8,128)(2,1)} %bitcast.315), kind=kOutput, calls=%fused_computation.29 | convolution fusion | flops 5308416000 | bytes 21619712 | tf_op jit(solution)/shard_map/dot_general | solution.py:392
  318.5 15.4 %convert_reduce_fusion = (f32[2304]{0:T(1024)}, bf16[1024,2304]{1,0:T(8,128)(2,1)}) fusion(f32[1024,2304]{1,0:T(8,128)} %get-tuple-element.188, f32[2304]{0:T(1024)S(1)} %copy-done.65, bf16[1024,1120]{1,0:T(8,128)(2,1)S(1)} %bitcast.296, bf16[2304,1120]{1,0:T(8,128)(2,1)S(1)} %bitcast.314), kind=kOutput, calls=%fused_computation.28 | convolution fusion | flops 5336725504 | bytes 21628928 | tf_op jit(solution)/shard_map/dot_general | solution.py:392
  333.9 9.8 %convolution_convert_fusion = bf16[2304,1120]{0,1:T(8,128)(2,1)} fusion(bf16[1024,2304]{1,0:T(8,128)(2,1)} %get-tuple-element.196, bf16[1024,1120]{1,0:T(8,128)(2,1)S(1)} %bitcast.293), kind=kOutput, calls=%fused_computation.10 | convolution fusion | flops 5287403520 | bytes 12173312 | tf_op jit(solution)/shard_map/dot_general | solution.py:392
  343.7 6.0 fusion.140
  356.2 9.0 %fusion.139 = f32[2,2,256,1120]{2,3,1,0:T(8,128)S(1)} fusion(bf16[2,2,256,2304]{3,2,1,0:T(8,128)(2,1)} %bitcast.319, bf16[2304,1120,1,1]{1,0,3,2:T(8,128)(2,1)} %bitcast.311), kind=kOutput, calls=%fused_computation.272 | convolution fusion | flops 5284823040 | bytes 14467072 | tf_op jit(solution)/shard_map/dot_general | solution.py:392
  393.6 6.3 convert_reduce_fusion.4
  403.7 9.7 %convolution_convert_fusion.1 = bf16[2304,1120]{0,1:T(8,128)(2,1)} fusion(bf16[1024,2304]{1,0:T(8,128)(2,1)} %get-tuple-element.187, bf16[1024,1120]{1,0:T(8,128)(2,1)S(1)} %bitcast.297), kind=kOutput, calls=%fused_computation.11 | convolution fusion | flops 5287403520 | bytes 12173312 | tf_op jit(solution)/shard_map/dot_general | solution.py:392
  416.6 8.5 %copy.148 = bf16[2304,1120]{1,0:T(8,128)(2,1)} copy(bf16[2304,1120]{0,1:T(8,128)(2,1)} %convolution_convert_fusion) | data formatting | bytes 10321920 | tf_op jit(solution)/shard_map/convert_element_type | solution.py:588
  425.2 8.6 %copy.147 = bf16[2304,1120]{1,0:T(8,128)(2,1)} copy(bf16[2304,1120]{0,1:T(8,128)(2,1)} %convolution_convert_fusion.1) | data formatting | bytes 10321920 | tf_op jit(solution)/shard_map/convert_element_type | solution.py:587
  456.7 13.3 %multiply_reduce_fusion = (f32[10,512]{1,0:T(8,128)S(1)}, f32[10,512,1024]{2,1,0:T(8,128)}) fusion(f32[10,512,1024]{2,1,0:T(8,128)} %copy-done.2, f32[10,512]{1,0:T(8,128)S(1)} %copy-done.49, bf16[10,1024,64]{1,2,0:T(8,128)(2,1)S(1)} %bitcast.280, bf16[10,1024,64]{1,2,0:T(8,128)(2,1)S(1)} %bitcast.263), kind=kOutput, calls=%fused_computation.1 | convolution fusion | flops 686812160 | bytes 43962368 | tf_op jit(solution)/shard_map/hqe,hke->hqk/dot_general | solution.py:459
  470.0 14.5 %multiply_convert_fusion = bf16[10,512,1024]{2,1,0:T(8,128)(2,1)S(1)} fusion(f32[10,512,1024]{2,1,0:T(8,128)} %get-tuple-element.190, f32[10,512,1024]{2,1,0:T(8,128)} %copy-done.2, f32[10,512]{1,0:T(8,128)S(1)} %get-tuple-element.189, f32[10,512]{1,0:T(8,128)S(1)} %copy-done.49), kind=kLoop, calls=%fused_computation | loop fusion | flops 20971520 | bytes 52469760 | tf_op jit(solution)/shard_map/convert_element_type | solution.py:461
  484.5 5.4 fusion.53
  513.7 9.1 %convert_reduce_fusion.2 = (f32[10,64]{1,0:T(8,128)S(1)}, bf16[10,1024,64]{1,2,0:T(8,128)(2,1)S(1)}) fusion(f32[10,512,1024]{2,1,0:T(8,128)} %copy-done.2, f32[10,512]{1,0:T(8,128)S(1)} %copy-done.49, bf16[10,1024,64]{1,2,0:T(8,128)(2,1)S(1)} %bitcast.264, f32[10,512,64]{1,2,0:T(8,128)S(1)} %copy-done.12), kind=kOutput, calls=%fused_computation.63 | convolution fusion | flops 684195200 | bytes 24283648 | tf_op jit(solution)/shard_map/hqk,hqe->hke/dot_general | solution.py:458
  534.1 6.0 concatenate.67
  540.1 7.2 convolution_convert_fusion.3
  547.3 5.5 copy.149
  552.9 7.9 %add_add_fusion = f32[1024,1120]{0,1:T(8,128)} fusion(f32[1024,1120]{0,1:T(8,128)} %fusion.59, f32[1024,1120]{0,1:T(8,128)} %fusion.58, bf16[1024,640]{0,1:T(8,128)(2,1)S(1)} %bitcast.256, bf16[320,1120]{0,1:T(8,128)(2,1)S(1)} %copy-done.20, bf16[320,1120]{0,1:T(8,128)(2,1)S(1)} %copy-done.19), kind=kOutput, calls=%fused_computation.49 | convolution fusion | flops 1473167360 | bytes 16506880 | tf_op jit(solution)/shard_map/dot_general | solution.py:392
  560.8 7.1 reshape.892
  578.4 6.0 concatenate.68
  584.4 5.8 convolution_convert_fusion.2
  597.5 5.6 copy.166
  603.1 5.7 pad_maximum_fusion.refs_2_
  615.9 152.1 %reduce_grads.1 = (f32[9,48,1120]{2,1,0:T(8,128)}, f32[16,1120]{1,0:T(8,128)}) custom-call(bf16[16,144,1120]{2,1,0:T(8,128)(2,1)} %bitcast.248, bf16[16,144,1120]{2,1,0:T(8,128)(2,1)} %bitcast.247, bf16[16,144,1120]{2,1,0:T(8,128)(2,1)} %pad_maximum_fusion.refs_2_, f32[16,1120]{1,0:T(8,128)} %pad.49.refs_3_), custom_call_target="tpu_custom_call" | custom-call | tf_op jit(solution)/shard_map/reduce_grads/pallas_call | solution.py:358
  783.9 5.5 collective-permute-done.7
  (335 shorter events, 235.1 us)
Async XLA Ops:
  0.7 10.0 %copy-start.36 = (bf16[2,1,256,1120]{2,3,1,0:T(8,128)(2,1)S(1)}, bf16[2,1,256,1120]{2,3,1,0:T(8,128)(2,1)}, u32[]{:S(2)}) copy-start(bf16[2,1,256,1120]{2,3,1,0:T(8,128)(2,1)} %param.27) | copy-start | bytes 3440644
  3.2 183.0 %copy-start.70 = (pred[1152]{0:T(1024)(128)(4,1)}, pred[1152]{0:T(1024)(128)(4,1)S(1)}, u32[]{:S(2)}) copy-start(pred[1152]{0:T(1024)(128)(4,1)S(1)} %fusion.98) | copy-start | bytes 3460
  3.3 183.0 %copy-start.66 = (s32[1152]{0:T(1024)}, s32[1152]{0:T(1024)S(1)}, u32[]{:S(2)}) copy-start(s32[1152]{0:T(1024)S(1)} %fusion.92) | copy-start | bytes 13828
  4.3 7.8 copy-start.37
  182.1 88.0 %copy-start.55 = (f32[4,256]{1,0:T(4,128)}, f32[4,256]{1,0:T(4,128)S(1)}, u32[]{:S(2)}) copy-start(f32[4,256]{1,0:T(4,128)S(1)} %get-tuple-element.179) | copy-start | bytes 12292
  200.1 6.0 copy-start.7
  211.7 23.2 %copy-start.2 = (f32[10,512,1024]{2,1,0:T(8,128)}, f32[10,512,1024]{2,1,0:T(8,128)S(1)}, u32[]{:S(2)}) copy-start(f32[10,512,1024]{2,1,0:T(8,128)S(1)} %get-tuple-element.184) | copy-start | bytes 62914564
  228.6 6.3 copy-start.21
  266.9 16.5 %collective-permute-start = (bf16[512,1120]{0,1:T(8,128)(2,1)}, bf16[512,1120]{0,1:T(8,128)(2,1)}, u32[]{:S(2)}, u32[]{:S(2)}) collective-permute-start(bf16[512,1120]{0,1:T(8,128)(2,1)} %copy.113), channel_id=1, source_target_pairs={{0,1},{1,0},{2,3},{3,2},{4,5},{5,4},{6,7},{7,6},{8,9},{9,8},{10,11... | collective-permute-start | bytes 3440648 | tf_op jit(solution)/shard_map/ppermute | solution.py:567
  279.3 5.8 copy-start.68
  290.9 11.4 %collective-permute-start.1 = (bf16[512,1120]{0,1:T(8,128)(2,1)}, bf16[512,1120]{0,1:T(8,128)(2,1)}, u32[]{:S(2)}, u32[]{:S(2)}) collective-permute-start(bf16[512,1120]{0,1:T(8,128)(2,1)} %copy.115), channel_id=1, source_target_pairs={{0,1},{1,0},{2,3},{3,2},{4,5},{5,4},{6,7},{7,6},{8,9},{9,8},{10,11... | collective-permute-start | bytes 3440648 | tf_op jit(solution)/shard_map/ppermute | solution.py:571
  294.3 5.6 copy-start.61
  304.0 14.4 %slice-start.3 = ((s8[5308416]{0:T(1024)(128)(4,1)}), s8[4194304]{0:T(1024)(128)(4,1)S(1)}, s32[]{:S(2)}) async-start(s8[5308416]{0:T(1024)(128)(4,1)} %bitcast.312), calls=%async_computation.3 | async-start | bytes 8388608
  306.4 12.0 %copy-start.30 = (bf16[4,256,1120]{2,1,0:T(8,128)(2,1)S(1)}, bf16[4,256,1120]{2,1,0:T(8,128)(2,1)}, u32[]{:S(2)}) copy-start(bf16[4,256,1120]{2,1,0:T(8,128)(2,1)} %get-tuple-element.89) | copy-start | bytes 6881284
  306.4 12.0 %slice-start.4 = ((s8[5308416]{0:T(1024)(128)(4,1)}), s8[1114112]{0:T(1024)(128)(4,1)S(1)}, s32[]{:S(2)}) async-start(s8[5308416]{0:T(1024)(128)(4,1)} %bitcast.312), calls=%async_computation.4 | async-start | bytes 2228224
  306.4 37.3 %slice-start.5 = ((s8[5308416]{0:T(1024)(128)(4,1)}), s8[4194304]{0:T(1024)(128)(4,1)S(1)}, s32[]{:S(2)}) async-start(s8[5308416]{0:T(1024)(128)(4,1)} %bitcast.316), calls=%async_computation.5 | async-start | bytes 8388608
  318.4 25.3 %slice-start.6 = ((s8[5308416]{0:T(1024)(128)(4,1)}), s8[1114112]{0:T(1024)(128)(4,1)S(1)}, s32[]{:S(2)}) async-start(s8[5308416]{0:T(1024)(128)(4,1)} %bitcast.316), calls=%async_computation.6 | async-start | bytes 2228224
  333.9 9.9 %copy-start.72 = (bf16[1024,2304]{1,0:T(8,128)(2,1)S(1)}, bf16[1024,2304]{1,0:T(8,128)(2,1)}, u32[]{:S(2)}) copy-start(bf16[1024,2304]{1,0:T(8,128)(2,1)} %get-tuple-element.196) | copy-start | bytes 14155780
  356.1 28.4 %collective-permute-start.4 = (bf16[512,1120]{0,1:T(8,128)(2,1)}, bf16[512,1120]{0,1:T(8,128)(2,1)}, u32[]{:S(2)}, u32[]{:S(2)}) collective-permute-start(bf16[512,1120]{0,1:T(8,128)(2,1)} %copy.131), channel_id=1, source_target_pairs={{0,1},{1,0},{2,3},{3,2},{4,5},{5,4},{6,7},{7,6},{8,9},{9,8},{10,11... | collective-permute-start | bytes 3440648 | tf_op jit(solution)/shard_map/ppermute | solution.py:567
  377.8 13.5 %collective-permute-start.2 = (bf16[512,1120]{0,1:T(8,128)(2,1)}, bf16[512,1120]{0,1:T(8,128)(2,1)}, u32[]{:S(2)}, u32[]{:S(2)}) collective-permute-start(bf16[512,1120]{0,1:T(8,128)(2,1)} %copy.124), channel_id=1, source_target_pairs={{0,1},{1,0},{2,3},{3,2},{4,5},{5,4},{6,7},{7,6},{8,9},{9,8},{10,11... | collective-permute-start | bytes 3440648 | tf_op jit(solution)/shard_map/ppermute | solution.py:567
  403.2 10.3 %copy-start.64 = (f32[2304]{0:T(1024)S(1)}, f32[2304]{0:T(1024)}, u32[]{:S(2)}) copy-start(f32[2304]{0:T(1024)} %get-tuple-element.195) | copy-start | bytes 27652
  403.2 30.8 %collective-permute-start.3 = (bf16[256,1120]{0,1:T(8,128)(2,1)}, bf16[256,1120]{0,1:T(8,128)(2,1)}, u32[]{:S(2)}, u32[]{:S(2)}) collective-permute-start(bf16[256,1120]{0,1:T(8,128)(2,1)} %bitcast.303), channel_id=1, source_target_pairs={{0,2},{1,3},{2,0},{3,1},{4,6},{5,7},{6,4},{7,5},{8,10},{9,11},{10,... | collective-permute-start | bytes 1720328 | tf_op jit(solution)/shard_map/ppermute | solution.py:637
  415.0 21.3 %collective-permute-start.5 = (bf16[512,1120]{0,1:T(8,128)(2,1)}, bf16[512,1120]{0,1:T(8,128)(2,1)S(1)}, u32[]{:S(2)}, u32[]{:S(2)}) collective-permute-start(bf16[512,1120]{0,1:T(8,128)(2,1)} %copy.133), channel_id=1, source_target_pairs={{0,1},{1,0},{2,3},{3,2},{4,5},{5,4},{6,7},{7,6},{8,9},{9,8},{10,11... | collective-permute-start | bytes 3440648 | tf_op jit(solution)/shard_map/ppermute | solution.py:571
  425.2 8.6 %copy-start.32 = (bf16[1,256,1120]{2,1,0:T(8,128)(2,1)S(1)}, bf16[1,256,1120]{2,1,0:T(8,128)(2,1)}, u32[]{:S(2)}) copy-start(bf16[1,256,1120]{2,1,0:T(8,128)(2,1)} %get-tuple-element.171) | copy-start | bytes 1720324
  534.1 6.0 copy-start.67
  534.1 6.0 copy-start.71
  577.9 30.9 %collective-permute-start.6 = (bf16[512,1120]{0,1:T(8,128)(2,1)}, bf16[512,1120]{0,1:T(8,128)(2,1)}, u32[]{:S(2)}, u32[]{:S(2)}) collective-permute-start(bf16[512,1120]{0,1:T(8,128)(2,1)} %copy.143), channel_id=1, source_target_pairs={{0,1},{1,0},{2,3},{3,2},{4,5},{5,4},{6,7},{7,6},{8,9},{9,8},{10,11... | collective-permute-start | bytes 3440648 | tf_op jit(solution)/shard_map/ppermute | solution.py:567
  603.1 7.6 copy-start.5
  603.1 7.6 copy-start.53
  615.9 155.0 %copy-start.69 = (f32[2,1,256,1]{2,1,0,3:T(1,128)S(1)}, f32[2,1,256,1]{2,1,0,3:T(1,128)}, u32[]{:S(2)}) copy-start(f32[2,1,256,1]{2,1,0,3:T(1,128)} %constant_dynamic-slice_fusion.6) | copy-start | bytes 6148
  776.0 13.4 %collective-permute-start.7 = (bf16[256,1120]{0,1:T(8,128)(2,1)}, bf16[256,1120]{0,1:T(8,128)(2,1)}, u32[]{:S(2)}, u32[]{:S(2)}) collective-permute-start(bf16[256,1120]{0,1:T(8,128)(2,1)} %bitcast.304), channel_id=1, source_target_pairs={{0,2},{1,3},{2,0},{3,1},{4,6},{5,7},{6,4},{7,5},{8,10},{9,11},{10,... | collective-permute-start | bytes 1720328 | tf_op jit(solution)/shard_map/ppermute | solution.py:637
  781.4 10.2 %copy-start.1 = (s32[2,1]{0,1:T(1,128)S(1)}, s32[2,1]{0,1:T(1,128)}, u32[]{:S(2)}) copy-start(s32[2,1]{0,1:T(1,128)} %param.28) | copy-start | bytes 28
  (56 other events, 160.3 us)

commit v2 on v0

v2 whole, which is shorter than its diff:
```python
import functools

import jax
import jax.numpy as jnp
import numpy as np
from jax import lax
from jax.experimental import pallas as pl
from jax.experimental.pallas import tpu as pltpu
from jax.sharding import PartitionSpec as P

HEAD_DIM = 56
PAD_DIM = 64
OUTER = 8
PIECE = 48
NORM_EPS = 1e-05
SCALE = HEAD_DIM ** (-0.5)
SCALE2 = SCALE * 1.4426950408889634
MESH = pl.DeviceIdType.MESH
BF16 = jnp.bfloat16
F32 = jnp.float32
BLOCK = 256
VMEM_LIMIT = 62 * 2**20


def place(inner):
    w = lax.axis_index("wide")
    n = lax.axis_index("narrow")
    outer = w // inner
    return outer // 2, outer % 2, n // 2, n % 2, w % inner


def device(inner, z, x, y, c, wi):
    return ((2 * z + x) * inner + wi, 2 * y + c)


def slab(y, x, z):
    return y * 8 + x * 4 + z


def remote(src, dst, send, recv, dev):
    return pltpu.make_async_remote_copy(
        src_ref=src, dst_ref=dst, send_sem=send, recv_sem=recv, device_id=dev, device_id_type=MESH
    )


def greet(devices):
    barrier = pltpu.get_barrier_semaphore()
    for dev in devices:
        pl.semaphore_signal(barrier, inc=1, device_id=dev, device_id_type=MESH)
    pl.semaphore_wait(barrier, len(devices))


class Links:
    def __init__(self, inner):
        z, x, y, c, wi = place(inner)
        self.z, self.x, self.y, self.c = z, x, y, c
        self.along = [device(inner, (z + d) % 4, x, y, c, wi) for d in (1, 2, 3)]
        self.xdev = device(inner, z, 1 - x, y, c, wi)
        self.ydev = device(inner, z, x, 1 - y, c, wi)
        self.cdev = device(inner, z, x, y, 1 - c, wi)
        self.pair = device(inner, z + 1 - 2 * (z % 2), x, y, c, wi)
        self.everyone = [*self.along, self.xdev, self.ydev, self.cdev]

    def back(self, d):
        return (self.z + 4 - d) % 4


dma = pltpu.SemaphoreType.DMA


def cut(ref, s, k):
    return ref.at[s, pl.ds(k * PIECE, PIECE)]


class LineGather:
    @staticmethod
    def sems(pieces):
        return [dma((pieces, 3)), dma((pieces, 3))]

    def __init__(self, links, own, out, at, sems):
        self.n, self.own, self.out, self.at = links, own, out, at
        self.zs, self.zr = sems

    def copy(self, k, d):
        src = self.own.at[pl.ds(k * PIECE, PIECE)]
        dst = cut(self.out, self.at(self.n.z), k)
        return remote(src, dst, self.zs.at[k, d - 1], self.zr.at[k, d - 1], self.n.along[d - 1])

    def came(self, k, d):
        v = cut(self.out, self.at(self.n.back(d)), k)
        return remote(v, v, self.zs.at[k, d - 1], self.zr.at[k, d - 1], self.n.along[d - 1])

    def start(self, k):
        for d in (1, 2, 3):
            self.copy(k, d).start()

    def wait(self, k):
        for d in (1, 2, 3):
            self.came(k, d).wait_recv()

    def sent(self, k):
        for d in (1, 2, 3):
            self.copy(k, d).wait_send()


class PlaneGather:
    @staticmethod
    def sems(pieces):
        return [dma((pieces, 4)) for _ in range(4)] + [dma((pieces, 2)) for _ in range(4)]

    def __init__(self, links, src, out, sems):
        self.n, self.src, self.out = links, src, out
        self.xs, self.xr, self.ys, self.yr, self.fxs, self.fxr, self.fys, self.fyr = sems

    def copy(self, k, d, over_x):
        n = self.n
        dst = cut(self.out, slab(n.y, n.x, n.back(d)), k)
        if over_x:
            return remote(self.src(k, d), dst, self.xs.at[k, d], self.xr.at[k, d], n.xdev)
        return remote(self.src(k, d), dst, self.ys.at[k, d], self.yr.at[k, d], n.ydev)

    def came(self, k, d, over_x):
        n = self.n
        if over_x:
            v = cut(self.out, slab(n.y, 1 - n.x, n.back(d)), k)
            return remote(v, v, self.xs.at[k, d], self.xr.at[k, d], n.xdev)
        v = cut(self.out, slab(1 - n.y, n.x, n.back(d)), k)
        return remote(v, v, self.ys.at[k, d], self.yr.at[k, d], n.ydev)

    def onward(self, k, d):
        n = self.n
        if d < 2:
            v = cut(self.out, slab(n.y, 1 - n.x, n.back(d)), k)
            return remote(v, v, self.fys.at[k, d], self.fyr.at[k, d], n.ydev)
        v = cut(self.out, slab(1 - n.y, n.x, n.back(d)), k)
        return remote(v, v, self.fxs.at[k, d - 2], self.fxr.at[k, d - 2], n.xdev)

    def crossed(self, k, d):
        n = self.n
        v = cut(self.out, slab(1 - n.y, 1 - n.x, n.back(d)), k)
        if d < 2:
            return remote(v, v, self.fys.at[k, d], self.fyr.at[k, d], n.ydev)
        return remote(v, v, self.fxs.at[k, d - 2], self.fxr.at[k, d - 2], n.xdev)

    def start(self, k, d):
        self.copy(k, d, True).start()
        self.copy(k, d, False).start()

    def forward(self, k):
        for d in (0, 1):
            self.came(k, d, True).wait_recv()
            self.onward(k, d).start()
            self.came(k, d + 2, False).wait_recv()
            self.onward(k, d + 2).start()

    def wait(self, k):
        for d in (0, 1):
            self.came(k, d + 2, True).wait_recv()
            self.came(k, d, False).wait_recv()
            self.crossed(k, d).wait_recv()
            self.crossed(k, d + 2).wait_recv()

    def sent(self, k):
        for d in range(4):
            self.copy(k, d, True).wait_send()
            self.copy(k, d, False).wait_send()
            self.onward(k, d).wait_send()


class PlaneReduce:
    @staticmethod
    def scratch(pieces, width):
        return [
            pltpu.VMEM((pieces, 4, PIECE, width), BF16),
            pltpu.VMEM((pieces, 4, PIECE, width), BF16),
            pltpu.VMEM((pieces, 4, PIECE, width), BF16),
            pltpu.VMEM((pieces, 4, PIECE, width), BF16),
        ] + [dma((pieces, 2)) for _ in range(6)]

    def __init__(self, links, part, out, scratch):
        self.n, self.part, self.out = links, part, out
        self.r1, self.rx, self.ry, self.mine = scratch[:4]
        self.s1, self.q1, self.s2, self.q2, self.s3, self.q3 = scratch[4:]

    def cut(self, k, s):
        return self.part.at[pl.ds(s, 2), pl.ds(k * PIECE, PIECE)]

    def load(self, k, s, count):
        return self.part[pl.ds(s, count), pl.ds(k * PIECE, PIECE)].astype(F32)

    def first(self, k):
        n, r = self.n, self.r1
        a = slab(1 - n.y, 1 - n.x, 0)
        return (
            remote(self.cut(k, a), r.at[k, pl.ds(0, 2)], self.s1.at[k, 0], self.q1.at[k, 0], n.ydev),
            remote(self.cut(k, a + 2), r.at[k, pl.ds(2, 2)], self.s1.at[k, 1], self.q1.at[k, 1], n.xdev),
        )

    def second(self, k):
        n = self.n
        ax, ay = slab(n.y, 1 - n.x, 2), slab(1 - n.y, n.x, 0)
        return (
            remote(self.cut(k, ax), self.rx.at[k, pl.ds(2, 2)], self.s2.at[k, 0], self.q2.at[k, 0], n.xdev),
            remote(self.cut(k, ay), self.ry.at[k, pl.ds(0, 2)], self.s2.at[k, 1], self.q2.at[k, 1], n.ydev),
        )

    def third(self, k):
        n, m = self.n, self.mine
        return (
            remote(m.at[k, pl.ds(0, 2)], self.rx.at[k, pl.ds(0, 2)], self.s3.at[k, 0], self.q3.at[k, 0], n.xdev),
            remote(m.at[k, pl.ds(2, 2)], self.ry.at[k, pl.ds(2, 2)], self.s3.at[k, 1], self.q3.at[k, 1], n.ydev),
        )

    def start(self, k):
        for cp in (*self.first(k), *self.second(k)):
            cp.start()

    def forward(self, k):
        n, f, t = self.n, self.first(k), self.third(k)
        f[0].wait_recv()
        self.mine[k, 0:2] = (self.load(k, slab(n.y, 1 - n.x, 0), 2) + self.r1[k, 0:2].astype(F32)).astype(BF16)
        t[0].start()
        f[1].wait_recv()
        self.mine[k, 2:4] = (self.load(k, slab(1 - n.y, n.x, 2), 2) + self.r1[k, 2:4].astype(F32)).astype(BF16)
        t[1].start()

    def finish(self, k):
        n = self.n
        for cp in (*self.second(k), *self.third(k)):
            cp.wait_recv()
        for j in (0, 2):
            self.out[pl.ds(j, 2), pl.ds(k * PIECE, PIECE)] = (
                self.load(k, slab(n.y, n.x, j), 2)
                + self.rx[k, j : j + 2].astype(F32)
                + self.ry[k, j : j + 2].astype(F32)
            ).astype(BF16)

    def sent(self, k):
        for cp in (*self.first(k), *self.second(k), *self.third(k)):
            cp.wait_send()


class LineReduce:
    @staticmethod
    def scratch(pieces, width):
        return [pltpu.VMEM((pieces, 3, PIECE, width), BF16), dma((pieces, 3)), dma((pieces, 3))]

    def __init__(self, links, line, out, used, scratch):
        self.n, self.line, self.out, self.used = links, line, out, used
        self.rz, self.sz, self.qz = scratch

    def copy(self, k, d):
        n = self.n
        src = cut(self.line, (n.z + d) % 4, k)
        return remote(src, self.rz.at[k, d - 1], self.sz.at[k, d - 1], self.qz.at[k, d - 1], n.along[d - 1])

    def start(self, k):
        for d in (1, 2, 3):
            self.copy(k, d).start()

    def finish(self, k):
        for d in (1, 2, 3):
            self.copy(k, d).wait_recv()
        total = self.line[self.n.z, pl.ds(k * PIECE, PIECE)].astype(F32)
        for d in range(3):
            total += self.rz[k, d].astype(F32)
        rows = min(PIECE, self.used - k * PIECE)
        self.out[pl.ds(k * PIECE, rows)] = total[:rows]

    def sent(self, k):
        for d in (1, 2, 3):
            self.copy(k, d).wait_send()


class Steps:
    def __init__(self, steps):
        self.steps = list(steps)

    def __call__(self, count=1):
        for _ in range(count):
            if self.steps:
                self.steps.pop(0)()

    def rest(self):
        self(len(self.steps))


def dot(a, b, dims):
    return lax.dot_general(a, b, (dims, ((), ())), preferred_element_type=F32)


def dot_nn(a, b):
    return dot(a, b, ((1,), (0,)))


def dot_nt(a, b):
    return dot(a, b, ((1,), (1,)))


def dot_tn(a, b):
    return dot(a, b, ((0,), (0,)))


def rows_at(i, size):
    return pl.ds(pl.multiple_of(i * size, size), size)


def loop(count, body):
    def step(i, carry):
        body(i)
        return carry

    lax.fori_loop(0, count, step, 0)


def norm_parts(v):
    center = v - jnp.mean(v, axis=-1, keepdims=True)
    rstd = lax.rsqrt(jnp.mean(center * center, axis=-1, keepdims=True) + NORM_EPS)
    return center * rstd, rstd


def norm_back(e, gain, xhat, rstd):
    eg = e * gain
    return rstd * (
        eg - jnp.mean(eg, axis=-1, keepdims=True) - xhat * jnp.mean(eg * xhat, axis=-1, keepdims=True)
    )


def gelu(u):
    t = jnp.tanh(0.7978845608 * (u + 0.044715 * u * u * u))
    h = 0.5 * u * (1.0 + t)
    d = 0.5 * (1.0 + t) + 0.5 * u * (1.0 - t * t) * 0.7978845608 * (1.0 + 3 * 0.044715 * u * u)
    return h, d


STRIP = 32


def k1_kernel(inner, pieces, *refs):
    it = iter(refs)
    take = lambda n: [next(it) for _ in range(n)]
    wa, wu, x_ref, g_ref, gain, shift = take(6)
    out_a, line_u, cells, normed, cot = take(5)
    za = take(2)
    pa = take(8)
    zu = take(2)
    ss, sr, ls = take(3)
    n = Links(inner)
    y, c = n.y, n.c
    greet(n.everyone)
    lga = LineGather(n, wa, out_a, lambda z: slab(y, n.x, z), za)
    lgu = LineGather(n, wu, line_u, lambda z: z, zu)

    def source(k, d):
        return wa.at[pl.ds(k * PIECE, PIECE)] if d == 0 else cut(out_a, slab(y, n.x, n.back(d)), k)

    pga = PlaneGather(n, source, out_a, pa)
    mine_a = pltpu.make_async_copy(wa, out_a.at[slab(y, n.x, n.z)], ls.at[0])
    mine_u = pltpu.make_async_copy(wu, line_u.at[n.z], ls.at[1])

    n_own, n_sib = 2 * y + c, 2 * y + 1 - c
    n_y, n_ys = 2 * (1 - y) + c, 2 * (1 - y) + 1 - c

    def swap(i, src, dst):
        return (
            pltpu.make_async_copy(src.at[y], dst.at[n_own], ls.at[2 + i]),
            remote(src.at[y], dst.at[n_own], ss.at[i, 0], sr.at[i, 0], n.cdev),
            remote(src.at[1 - y], dst.at[n_own], ss.at[i, 1], sr.at[i, 1], n.ydev),
            remote(dst.at[n_y], dst.at[n_y], ss.at[i, 1], sr.at[i, 1], n.ydev),
            remote(dst.at[n_y], dst.at[n_y], ss.at[i, 2], sr.at[i, 2], n.cdev),
            remote(dst.at[n_sib], dst.at[n_sib], ss.at[i, 0], sr.at[i, 0], n.cdev),
            remote(dst.at[n_ys], dst.at[n_ys], ss.at[i, 2], sr.at[i, 2], n.cdev),
        )

    xp, gp = swap(0, x_ref, cells), swap(1, g_ref, cot)

    def begin(p):
        for cp in p[:3]:
            cp.start()

    def middle(p):
        p[3].wait_recv()
        p[4].start()

    def end(p):
        p[0].wait()
        p[5].wait_recv()
        p[6].wait_recv()

    def done(p):
        for cp in (p[1], p[2], p[4]):
            cp.wait_send()

    for k in range(pieces):
        lga.start(k)
    for k in range(pieces):
        pga.start(k, 0)
    begin(xp)
    mine_a.start()
    mine_u.start()
    for k in range(pieces):
        for d in (1, 2, 3):
            lga.came(k, d).wait_recv()
            pga.start(k, d)
        if k == 0:
            for kk in range(pieces):
                lgu.start(kk)
            middle(xp)
        if k > 0:
            pga.forward(k - 1)
    begin(gp)
    end(xp)

    def norm(i):
        for b in range(4):
            r = rows_at(i, STRIP)
            xhat, _ = norm_parts(cells[b, r].astype(F32))
            normed[b, r] = (xhat * gain[...] + shift[...]).astype(BF16)

    loop(cells.shape[1] // STRIP, norm)
    pga.forward(pieces - 1)
    middle(gp)
    for k in range(pieces):
        pga.wait(k)
        lgu.wait(k)
    end(gp)
    mine_a.wait()
    mine_u.wait()
    for k in range(pieces):
        lga.sent(k)
        lgu.sent(k)
        pga.sent(k)
    done(xp)
    done(gp)


def k2_kernel(inner, pieces, *refs):
    it = iter(refs)
    take = lambda n: [next(it) for _ in range(n)]
    g_a, order, normed, cells, bias_qkv, bias_out, gain, shift, cell_len, line_u, wd = take(11)
    out_u, line_d, qkv, mixed, lse, middle, normed2, wa = take(8)
    bias, own, send, got = take(4)
    pu = take(8)
    zd = take(2)
    es, er, ls = take(3)
    n = Links(inner)
    y, c = n.y, n.c
    greet(n.everyone)
    lgd = LineGather(n, wd, line_d, lambda z: z, zd)
    pgu = PlaneGather(n, lambda k, d: cut(line_u, n.back(d), k), out_u, pu)
    locals_ = [
        pltpu.make_async_copy(line_u, out_u.at[pl.ds(slab(y, n.x, 0), 4)], ls.at[0]),
        pltpu.make_async_copy(wd, line_d.at[n.z], ls.at[1]),
    ]
    for k in range(pieces):
        for d in range(4):
            pgu.start(k, d)
    for k in range(pieces):
        lgd.start(k)
    for cp in locals_:
        cp.start()
    steps = Steps([functools.partial(pgu.forward, k) for k in range(pieces)])

    heads = order.shape[0] // (4 * PAD_DIM)
    part = 2 * heads * PAD_DIM
    for yy in range(2):
        for p in range(4):
            m = dot_nn(order[p * heads * PAD_DIM : (p + 1) * heads * PAD_DIM], g_a[yy]).astype(BF16)
            for h in range(heads):
                wa[pl.ds(p * part + h * 2 * PAD_DIM + yy * PAD_DIM, PAD_DIM)] = m[h * PAD_DIM : (h + 1) * PAD_DIM]

    blocks = qkv.shape[0] // BLOCK
    total = blocks * BLOCK

    def project(t):
        r = rows_at(t, BLOCK)
        a = normed[r]
        for p in range(3):
            w = wa[p * part : (p + 1) * part]
            cols = slice(p * part, (p + 1) * part)
            qkv[r, cols] = (dot_nt(a, w) + bias_qkv[:, cols]).astype(BF16)

    loop(blocks, project)
    steps()
    key = lax.broadcasted_iota(jnp.int32, (BLOCK, total), 1)
    row = lax.broadcasted_iota(jnp.int32, (BLOCK, total), 0)
    for i in range(blocks):
        ok = (key <= row + i * BLOCK) & (key < cell_len[0])
        bias[i] = jnp.where(ok, 0.0, -1e30)
    lane = lax.broadcasted_iota(jnp.int32, (BLOCK, 2 * PAD_DIM), 1)
    low = lane < PAD_DIM
    lse[...] = jnp.zeros_like(lse)

    for i in range(blocks):
        r = slice(i * BLOCK, (i + 1) * BLOCK)
        end = (i + 1) * BLOCK

        def attend(j, r=r, end=end, i=i):
            def cols(p):
                return pl.ds(pl.multiple_of(p * part + j * 2 * PAD_DIM, 2 * PAD_DIM), 2 * PAD_DIM)

            q, k, v = qkv[r, cols(0)], qkv[:end, cols(1)], qkv[:end, cols(2)]
            outs = []
            for half in range(2):
                qm = jnp.where(low if half == 0 else ~low, q, jnp.zeros_like(q))
                s = dot_nt(qm, k) * SCALE2 + bias[i, :, :end]
                m = jnp.max(s, axis=-1, keepdims=True)
                e = jnp.exp2(s - m)
                t = jnp.sum(e, axis=-1, keepdims=True)
                p = (e * (1.0 / t)).astype(BF16)
                outs.append(dot_nn(p, v))
                lse[r] = jnp.where(lane == 2 * j + half, m + jnp.log2(t), lse[r])
            mixed[r, cols(0)] = jnp.where(low, outs[0], outs[1]).astype(BF16)

        loop(heads, attend)
        steps()

    wo = wa.at[pl.ds(3 * part, part)]

    def swap(i, h):
        return remote(send.at[h], got.at[h], es.at[i, h], er.at[i, h], n.cdev)

    def n2(h):
        v = normed2.at[pl.ds(pl.multiple_of((2 * h + c) * BLOCK, BLOCK), BLOCK)]
        return remote(v, v, es.at[1, h], er.at[1, h], n.cdev)

    def n2_in(h):
        v = normed2.at[pl.ds(pl.multiple_of((2 * h + 1 - c) * BLOCK, BLOCK), BLOCK)]
        return remote(v, v, es.at[1, h], er.at[1, h], n.cdev)

    for h in range(2):
        send[h] = dot_nn(mixed[rows_at(2 * h + 1 - c, BLOCK)], wo[...]).astype(BF16)
        swap(0, h).start()
    for h in range(2):
        own[h] = dot_nn(mixed[rows_at(2 * h + c, BLOCK)], wo[...])
    for h in range(2):
        swap(0, h).wait_recv()

        def finish(i, h=h):
            r = rows_at(i, STRIP)
            x = cells[2 * h + c, r].astype(F32)
            mid = x + own[h, r] + got[h, r].astype(F32) + bias_out[...]
            middle[h, r] = mid
            xhat, _ = norm_parts(mid)
            start = pl.multiple_of((2 * h + c) * BLOCK + i * STRIP, STRIP)
            normed2[pl.ds(start, STRIP)] = (xhat * gain[...] + shift[...]).astype(BF16)

        loop(BLOCK // STRIP, finish)
        n2(h).start()
    steps.rest()
    for h in range(2):
        n2_in(h).wait_recv()
    for k in range(pieces):
        pgu.wait(k)
        lgd.wait(k)
    for cp in locals_:
        cp.wait()
    for h in range(2):
        swap(0, h).wait_send()
        n2(h).wait_send()
    for k in range(pieces):
        pgu.sent(k)
        lgd.sent(k)


CHUNK = 768
WIDE = 256


def k3_kernel(inner, pieces, *refs):
    it = iter(refs)
    take = lambda n: [next(it) for _ in range(n)]
    normed2, wu, bias_up, cot, line_d = take(5)
    out_d, hidden, slope, part_d = take(4)
    pd = take(8)
    (ls,) = take(1)
    n = Links(inner)
    greet([n.xdev, n.ydev])
    pgd = PlaneGather(n, lambda k, d: cut(line_d, n.back(d), k), out_d, pd)
    mine = pltpu.make_async_copy(line_d, out_d.at[pl.ds(slab(n.y, n.x, 0), 4)], ls.at[0])
    for k in range(pieces):
        for d in range(4):
            pgd.start(k, d)
    mine.start()
    steps = Steps([functools.partial(pgd.forward, k) for k in range(pieces)])
    units = hidden.shape[1]

    def up(t):
        r = rows_at(t, BLOCK)
        a = normed2[r]
        for q in range(units // CHUNK):
            cols = slice(q * CHUNK, (q + 1) * CHUNK)
            h, d = gelu(dot_nt(a, wu[cols]) + bias_up[:, cols])
            hidden[r, cols] = h.astype(BF16)
            slope[r, cols] = d.astype(BF16)

    loop(hidden.shape[0] // BLOCK, up)
    steps()

    def grad(q):
        part_d[rows_at(q, WIDE)] = dot_tn(hidden[:, rows_at(q, WIDE)], cot[...]).astype(BF16)

    loop(units // WIDE, grad)
    steps.rest()
    for k in range(pieces):
        pgd.wait(k)
    mine.wait()
    for k in range(pieces):
        pgd.sent(k)


def k4_kernel(inner, pieces, *refs):
    it = iter(refs)
    take = lambda n: [next(it) for _ in range(n)]
    hidden, slope, wd, wu, cot, normed2, middle, mixed, wo, bias_down, gain, part_d = take(12)
    cells_out, line_d, part_u, part_o, grad_mid, grad_mixed, sums, sum_up = take(8)
    grad_up, grad_att, own, send, got, outb = take(6)
    rd = take(10)
    es, er, ys, yr, ls = take(5)
    n = Links(inner)
    y, c = n.y, n.c
    greet([n.xdev, n.ydev, n.cdev])
    red = PlaneReduce(n, part_d, line_d, rd)
    for k in range(pieces):
        red.start(k)
    steps = Steps(
        [functools.partial(red.forward, k) for k in range(pieces)]
        + [functools.partial(red.finish, k) for k in range(pieces)]
    )
    units = hidden.shape[1]
    load = pltpu.make_async_copy(hidden, grad_up, ls.at[1])
    load.start()
    load.wait()

    def swap(i, h):
        return remote(send.at[i, h], got.at[i, h], es.at[i, h], er.at[i, h], n.cdev)

    for h in range(2):
        send[0, h] = dot_nn(grad_up[rows_at(2 * h + 1 - c, BLOCK)], wd[...]).astype(BF16)
        swap(0, h).start()
    for h in range(2):
        own[h] = dot_nn(grad_up[rows_at(2 * h + c, BLOCK)], wd[...])
    steps()
    for h in range(2):
        swap(0, h).wait_recv()

        def finish(i, h=h):
            r = rows_at(i, STRIP)
            outb[h, r] = (middle[h, r] + own[h, r] + got[0, h, r].astype(F32) + bias_down[...]).astype(BF16)

        loop(BLOCK // STRIP, finish)
    keep = pltpu.make_async_copy(outb.at[y], cells_out.at[y], ls.at[0])
    over = remote(outb.at[1 - y], cells_out.at[y], ys.at[0], yr.at[0], n.ydev)
    over_in = remote(outb.at[1 - y], cells_out.at[1 - y], ys.at[0], yr.at[0], n.ydev)
    keep.start()
    over.start()

    sum_up[...] = jnp.zeros_like(sum_up)

    def back(t):
        r = rows_at(t, BLOCK)
        a = cot[r]
        for q in range(units // CHUNK):
            cols = slice(q * CHUNK, (q + 1) * CHUNK)
            g = (dot_nt(a, wd[cols]) * slope[r, cols].astype(F32)).astype(BF16)
            grad_up[r, cols] = g
            sum_up[:, cols] += jnp.sum(g.astype(F32), axis=0, keepdims=True)

    loop(hidden.shape[0] // BLOCK, back)
    steps()
    for h in range(2):
        send[1, h] = dot_nn(grad_up[rows_at(2 * h + 1 - c, BLOCK)], wu[...]).astype(BF16)
        swap(1, h).start()
    for h in range(2):
        own[h] = dot_nn(grad_up[rows_at(2 * h + c, BLOCK)], wu[...])
    steps()
    sums[...] = jnp.zeros_like(sums)

    def att(h):
        v = grad_att.at[pl.ds(pl.multiple_of((2 * h + c) * BLOCK, BLOCK), BLOCK)]
        return remote(v, v, es.at[2, h], er.at[2, h], n.cdev)

    def att_in(h):
        v = grad_att.at[pl.ds(pl.multiple_of((2 * h + 1 - c) * BLOCK, BLOCK), BLOCK)]
        return remote(v, v, es.at[2, h], er.at[2, h], n.cdev)

    for h in range(2):
        swap(1, h).wait_recv()

        def finish2(i, h=h):
            r = rows_at(i, STRIP)
            at = pl.ds(pl.multiple_of((2 * h + c) * BLOCK + i * STRIP, STRIP), STRIP)
            e = own[h, r] + got[1, h, r].astype(F32)
            xhat, rstd = norm_parts(middle[h, r])
            top = cot[at].astype(F32)
            g = top + norm_back(e, gain[...], xhat, rstd)
            grad_mid[h, r] = g
            low = g.astype(BF16)
            grad_att[at] = low
            sums[0:1] += jnp.sum(e * xhat, axis=0, keepdims=True)
            sums[1:2] += jnp.sum(e, axis=0, keepdims=True)
            sums[2:3] += jnp.sum(low.astype(F32), axis=0, keepdims=True)
            sums[3:4] += jnp.sum(top, axis=0, keepdims=True)

        loop(BLOCK // STRIP, finish2)
        att(h).start()
    steps()

    def grad(q):
        part_u[rows_at(q, WIDE)] = dot_tn(grad_up[:, rows_at(q, WIDE)], normed2[...]).astype(BF16)

    loop(units // WIDE, grad)
    steps()
    for h in range(2):
        att_in(h).wait_recv()

    def to_heads(t):
        r = rows_at(t, BLOCK)
        grad_mixed[r] = dot_nt(grad_att[r], wo[...]).astype(BF16)

    loop(hidden.shape[0] // BLOCK, to_heads)
    part_o[...] = dot_tn(mixed[...], grad_att[...]).astype(BF16)
    steps.rest()
    keep.wait()
    over_in.wait_recv()
    over.wait_send()
    for h in range(2):
        swap(0, h).wait_send()
        swap(1, h).wait_send()
        att(h).wait_send()
    for k in range(pieces):
        red.sent(k)


def k5_kernel(inner, pieces, used, *refs):
    it = iter(refs)
    take = lambda n: [next(it) for _ in range(n)]
    qkv, lse, grad_mixed, normed, part_o, order_t, cell_len, part_u, line_d = take(9)
    grads, part_a, line_u, grad_d, sums = take(5)
    bias, gk, gv, stack, lse_t = take(5)
    ru = take(10)
    rz = take(3)
    n = Links(inner)
    greet([*n.along, n.xdev, n.ydev])
    red = PlaneReduce(n, part_u, line_u, ru)
    line = LineReduce(n, line_d, grad_d, used, rz)
    for k in range(pieces):
        red.start(k)
        line.start(k)
    steps = Steps(
        [functools.partial(red.forward, k) for k in range(pieces)]
        + [functools.partial(line.finish, k) for k in range(pieces)]
        + [functools.partial(red.finish, k) for k in range(pieces)]
    )
    total = qkv.shape[0]
    part = qkv.shape[1] // 3
    blocks = total // BLOCK
    heads = part // (2 * PAD_DIM)
    key = lax.broadcasted_iota(jnp.int32, (total, BLOCK), 0)
    row = lax.broadcasted_iota(jnp.int32, (total, BLOCK), 1)
    for i in range(blocks):
        ok = (key <= row + i * BLOCK) & (key < cell_len[0])
        bias[i] = jnp.where(ok, 0.0, -1e30)
    lse_t[...] = jnp.transpose(lse[...])
    low = lax.broadcasted_iota(jnp.int32, (BLOCK, 2 * PAD_DIM), 1) < PAD_DIM
    gk[...] = jnp.zeros_like(gk)
    gv[...] = jnp.zeros_like(gv)

    for i in range(blocks):
        r = slice(i * BLOCK, (i + 1) * BLOCK)
        end = (i + 1) * BLOCK
        wide_low = lax.broadcasted_iota(jnp.int32, (end, 2 * PAD_DIM), 1) < PAD_DIM

        def attend(j, r=r, end=end, i=i, wide_low=wide_low):
            def cols(p):
                return pl.ds(pl.multiple_of(p * part + j * 2 * PAD_DIM, 2 * PAD_DIM), 2 * PAD_DIM)

            q, k, v = qkv[r, cols(0)], qkv[:end, cols(1)], qkv[:end, cols(2)]
            g = grad_mixed[r, cols(0)]
            zero = jnp.zeros_like(q)
            gqs, gks, gvs = [], [], []
            for half in range(2):
                here = low if half == 0 else ~low
                s = dot_nt(k, jnp.where(here, q, zero)) * SCALE2 + bias[i, :end]
                p = jnp.exp2(s - lse_t[pl.ds(2 * j + half, 1), r])
                gp = dot_nt(v, jnp.where(here, g, zero))
                inner_sum = jnp.sum(p * gp, axis=0, keepdims=True)
                ds = (p * (gp - inner_sum)).astype(BF16)
                gvs.append(dot_nn(p.astype(BF16), g))
                gks.append(dot_nn(ds, q))
                gqs.append(dot_tn(ds, k))
            gk[:end, cols(0)] += jnp.where(wide_low, gks[0], gks[1])
            gv[:end, cols(0)] += jnp.where(wide_low, gvs[0], gvs[1])
            grads[r, cols(0)] = (jnp.where(low, gqs[0], gqs[1]) * SCALE).astype(BF16)

        loop(heads, attend)
        steps()

    def settle(t):
        r = rows_at(t, BLOCK)
        grads[r, part : 2 * part] = (gk[r] * SCALE).astype(BF16)
        grads[r, 2 * part :] = gv[r].astype(BF16)

    loop(blocks, settle)
    steps()
    sums[...] = jnp.sum(grads[...].astype(F32), axis=0, keepdims=True)
    for p in range(4):
        for h in range(heads):
            if p < 3:
                at = p * part + h * 2 * PAD_DIM
                m = dot_tn(grads[:, at : at + 2 * PAD_DIM], normed[...]).astype(BF16)
            else:
                m = part_o[h * 2 * PAD_DIM : (h + 1) * 2 * PAD_DIM]
            for yy in range(2):
                stack[yy, pl.ds(p * heads * PAD_DIM + h * PAD_DIM, PAD_DIM)] = m[yy * PAD_DIM : (yy + 1) * PAD_DIM]
    steps()
    size = order_t.shape[0]
    for yy in range(2):

        def reorder(i, yy=yy):
            part_a[yy, rows_at(i, size // 3)] = dot_nn(order_t[rows_at(i, size // 3)], stack[yy]).astype(BF16)

        loop(3, reorder)
    steps.rest()
    for k in range(pieces):
        red.sent(k)
        line.sent(k)


def k6_kernel(inner, pieces, used, *refs):
    it = iter(refs)
    take = lambda n: [next(it) for _ in range(n)]
    grads, wa, cells, grad_mid, gain, small, part_a, line_u = take(8)
    grad_in, grad_a, grad_u, small_out = take(4)
    own, send, got, outb, line_a, acc, inbox = take(7)
    ra = take(10)
    rzu = take(3)
    rza = take(3)
    es, er, ys, yr, ls, sa, qa = take(7)
    n = Links(inner)
    y, c = n.y, n.c
    greet(n.everyone)
    red = PlaneReduce(n, part_a, line_a, ra)
    linu = LineReduce(n, line_u, grad_u, used, rzu)
    lina = LineReduce(n, line_a, grad_a, used, rza)
    for k in range(pieces):
        red.start(k)
        linu.start(k)

    def swap(h):
        return remote(send.at[h], got.at[h], es.at[h], er.at[h], n.cdev)

    w = wa.at[pl.ds(0, grads.shape[1])]
    for h in range(2):
        send[h] = dot_nn(grads[rows_at(2 * h + 1 - c, BLOCK)], w[...]).astype(BF16)
        swap(h).start()
    for h in range(2):
        own[h] = dot_nn(grads[rows_at(2 * h + c, BLOCK)], w[...])
    red.forward(0)
    acc[0] = small[...]
    for h in range(2):
        swap(h).wait_recv()

        def finish(i, h=h):
            r = rows_at(i, STRIP)
            e = own[h, r] + got[h, r].astype(F32)
            xhat, rstd = norm_parts(cells[2 * h + c, r].astype(F32))
            outb[h, r] = (grad_mid[h, r] + norm_back(e, gain[...], xhat, rstd)).astype(BF16)
            acc[0, 0:1] += jnp.sum(e * xhat, axis=0, keepdims=True)
            acc[0, 1:2] += jnp.sum(e, axis=0, keepdims=True)

        loop(BLOCK // STRIP, finish)
    keep = pltpu.make_async_copy(outb.at[y], grad_in.at[y], ls.at[0])
    over = remote(outb.at[1 - y], grad_in.at[y], ys.at[0], yr.at[0], n.ydev)
    over_in = remote(outb.at[1 - y], grad_in.at[1 - y], ys.at[0], yr.at[0], n.ydev)
    keep.start()
    over.start()
    peers = [n.cdev, n.xdev, n.ydev, n.pair, n.along[1]]

    def small_copy(i):
        return remote(acc.at[i], inbox.at[i], sa.at[i], qa.at[i], peers[i])

    def small_step(i):
        if i > 0:
            small_copy(i - 1).wait_recv()
            acc[i] = acc[i - 1] + inbox[i - 1]
        if i < 5:
            small_copy(i).start()

    small_step(0)
    red.forward(1)
    small_step(1)
    red.finish(0)
    lina.start(0)
    small_step(2)
    red.forward(2)
    small_step(3)
    for k in range(pieces):
        linu.finish(k)
    small_step(4)
    red.finish(1)
    lina.start(1)
    small_step(5)
    small_out[...] = acc[5]
    lina.finish(0)
    red.finish(2)
    lina.start(2)
    lina.finish(1)
    lina.finish(2)
    keep.wait()
    over_in.wait_recv()
    over.wait_send()
    for h in range(2):
        swap(h).wait_send()
    for i in range(5):
        small_copy(i).wait_send()
    for k in range(pieces):
        red.sent(k)
        linu.sent(k)
        lina.sent(k)


ANY = pl.BlockSpec(memory_space=pl.ANY)
VM = pl.BlockSpec(memory_space=pltpu.VMEM)
SM = pl.BlockSpec(memory_space=pltpu.SMEM)


def call(kernel, ident, name, outs, ins, scratch):
    return pl.pallas_call(
        kernel,
        out_shape=[jax.ShapeDtypeStruct(s, d) for s, d, _ in outs],
        in_specs=[s for _, s in ins],
        out_specs=[s for _, _, s in outs],
        scratch_shapes=scratch,
        compiler_params=pltpu.CompilerParams(
            collective_id=ident, has_side_effects=True, vmem_limit_bytes=VMEM_LIMIT
        ),
        name=name,
    )(*[a for a, _ in ins])


def order_matrix(rows, heads):
    m = np.zeros((4 * heads * PAD_DIM, OUTER * rows), np.float32)
    each = HEAD_DIM // OUTER
    for x in range(2):
        for z in range(4):
            w = 2 * z + x
            for g in range(4 * heads):
                part, head = (g % 3, g // 3) if g < 3 * heads else (3, g - 3 * heads)
                for e in range(each):
                    m[part * heads * PAD_DIM + head * PAD_DIM + w * each + e, (x * 4 + z) * rows + g * each + e] = 1
    return m


def pad_rows(a, rows):
    return jnp.pad(a, ((0, rows - a.shape[0]), (0, 0)))


def on_device(
    cells_in, lengths, w_qkv, w_out, w_up, w_down, ln1_gain, ln1_shift, bias_qv, bias_out,
    ln2_gain, ln2_shift, bias_up, bias_down, cotangent,
):
    wide = lax.axis_size("wide")
    inner = wide // OUTER
    shards = [w_qkv, w_out, w_up, w_down]
    if inner > 1:
        groups = [[o * inner + i for i in range(inner)] for o in range(OUTER)]
        shards = [
            lax.all_gather(s, "wide", axis=1, tiled=True, axis_index_groups=groups) for s in shards
        ]
    width = cells_in.shape[3]
    local_rows = cells_in.shape[2]
    total = 4 * local_rows
    heads = width // HEAD_DIM // 4
    part = 2 * heads * PAD_DIM
    n = lax.axis_index("narrow")
    y, c = n // 2, n % 2
    w_a = jnp.concatenate([shards[0].reshape(-1, width), shards[1].reshape(-1, width)], axis=0)
    used = w_a.shape[0]
    rows = -(-used // PIECE) * PIECE
    pieces = rows // PIECE
    w_a = pad_rows(w_a, rows)
    w_u = pad_rows(shards[2].reshape(-1, width), rows)
    w_d = pad_rows(shards[3].reshape(-1, width), rows)
    units = 16 * rows
    order_np = order_matrix(rows, heads)
    order = jnp.asarray(order_np, BF16)
    order_t = jnp.asarray(np.ascontiguousarray(order_np.T), BF16)

    def line(v):
        return v.reshape(1, -1)

    def pick_heads(b):
        b = b.reshape(2, 2, heads, HEAD_DIM)
        b = lax.dynamic_index_in_dim(b, c, axis=1, keepdims=False)
        b = jnp.pad(b, ((0, 0), (0, 0), (0, PAD_DIM - HEAD_DIM)))
        return b.transpose(1, 0, 2).reshape(-1)

    zero = jnp.zeros((part,), F32)
    bias_qkv = line(jnp.concatenate([pick_heads(bias_qv[:width]), zero, pick_heads(bias_qv[width:])]))
    b_u = bias_up.reshape(2, 2, used, 4, 2)
    b_u = lax.dynamic_index_in_dim(b_u, c, axis=1, keepdims=False).transpose(0, 3, 2, 1)
    b_u = line(jnp.pad(b_u, ((0, 0), (0, 0), (0, 0), (0, rows - used))))
    cell_len = lax.dynamic_slice_in_dim(lengths[:, 0], y, 1)

    slabs = (16, rows, width)
    lines = (4, rows, width)
    g_a, line_u, cells, normed, cot = call(
        functools.partial(k1_kernel, inner, pieces), 0, "gather_first",
        [(slabs, BF16, ANY), (lines, BF16, ANY), ((4, local_rows, width), BF16, VM),
         ((4, local_rows, width), BF16, VM), ((4, local_rows, width), BF16, ANY)],
        [(w_a, ANY), (w_u, ANY), (cells_in[:, 0], ANY), (cotangent[:, 0], ANY),
         (line(ln1_gain), VM), (line(ln1_shift), VM)],
        [*LineGather.sems(pieces), *PlaneGather.sems(pieces), *LineGather.sems(pieces),
         dma((2, 3)), dma((2, 3)), dma((4,))],
    )
    normed = normed.reshape(total, width)
    cot = cot.reshape(total, width)
    half = (2, BLOCK, width)
    g_u, line_d, qkv, mixed, lse, middle, normed2, wa = call(
        functools.partial(k2_kernel, inner, pieces), 1, "attend",
        [(slabs, BF16, ANY), (lines, BF16, ANY), ((total, 3 * part), BF16, VM), ((total, part), BF16, VM),
         ((total, 2 * PAD_DIM), F32, VM), (half, F32, VM), ((total, width), BF16, VM), ((4 * part, width), BF16, VM)],
        [(g_a.reshape(2, OUTER * rows, width), VM), (order, VM), (normed, VM), (cells, VM), (bias_qkv, VM),
         (line(bias_out), VM), (line(ln2_gain), VM), (line(ln2_shift), VM), (cell_len, SM), (line_u, ANY), (w_d, ANY)],
        [pltpu.VMEM((total // BLOCK, BLOCK, total), F32), pltpu.VMEM(half, F32), pltpu.VMEM(half, BF16),
         pltpu.VMEM(half, BF16), *PlaneGather.sems(pieces), *LineGather.sems(pieces),
         dma((2, 2)), dma((2, 2)), dma((2,))],
    )
    wu = g_u.reshape(units, width)
    g_d, hidden, slope, part_d = call(
        functools.partial(k3_kernel, inner, pieces), 2, "hidden_units",
        [(slabs, BF16, ANY), ((total, units), BF16, VM), ((total, units), BF16, VM), ((units, width), BF16, VM)],
        [(normed2, VM), (wu, VM), (b_u, VM), (cot, VM), (line_d, ANY)],
        [*PlaneGather.sems(pieces), dma((1,))],
    )
    wd = g_d.reshape(units, width)
    two = (2, 2, BLOCK, width)
    cells_out, line_gd, part_u, part_o, grad_mid, grad_mixed, sums4, sum_up = call(
        functools.partial(k4_kernel, inner, pieces), 3, "hidden_units_back",
        [((2, local_rows, width), BF16, ANY), (lines, BF16, VM), ((units, width), BF16, VM), ((part, width), BF16, VM),
         (half, F32, VM), ((total, part), BF16, VM), ((8, width), F32, VM), ((1, units), F32, VM)],
        [(hidden, ANY), (slope, VM), (wd, VM), (wu, VM), (cot, VM), (normed2, VM), (middle, VM), (mixed, VM),
         (wa[3 * part :], VM), (line(bias_down), VM), (line(ln2_gain), VM), (part_d.reshape(slabs), VM)],
        [pltpu.VMEM((total, units), BF16), pltpu.VMEM((total, width), BF16), pltpu.VMEM(half, F32),
         pltpu.VMEM(two, BF16), pltpu.VMEM(two, BF16), pltpu.VMEM(half, BF16),
         *PlaneReduce.scratch(pieces, width), dma((3, 2)), dma((3, 2)), dma((1,)), dma((1,)), dma((2,))],
    )
    grads, part_a, line_gu, grad_d, sum_qkv = call(
        functools.partial(k5_kernel, inner, pieces, used), 4, "attend_back",
        [((total, 3 * part), BF16, VM), ((2, OUTER * rows, width), BF16, VM), (lines, BF16, VM),
         ((used, width), F32, VM), ((1, 3 * part), F32, VM)],
        [(qkv, VM), (lse, VM), (grad_mixed, VM), (normed, VM), (part_o, VM), (order_t, VM), (cell_len, SM),
         (part_u.reshape(slabs), VM), (line_gd, VM)],
        [pltpu.VMEM((total // BLOCK, total, BLOCK), F32), pltpu.VMEM((total, part), F32), pltpu.VMEM((total, part), F32),
         pltpu.VMEM((2, 4 * heads * PAD_DIM, width), BF16), pltpu.VMEM((2 * PAD_DIM, total), F32),
         *PlaneReduce.scratch(pieces, width), *LineReduce.scratch(pieces, width)],
    )

    def put_heads(s):
        s = s.reshape(heads, 2, PAD_DIM)[..., :HEAD_DIM].transpose(1, 0, 2)[:, None]
        zero = jnp.zeros_like(s)
        return jnp.where(c == 0, jnp.concatenate([s, zero], 1), jnp.concatenate([zero, s], 1)).reshape(-1)

    def put_hidden(s):
        s = s.reshape(2, 2, 4, rows)[..., :used].transpose(0, 3, 2, 1).reshape(2, 1, -1)
        zero = jnp.zeros_like(s)
        return jnp.where(c == 0, jnp.concatenate([s, zero], 1), jnp.concatenate([zero, s], 1)).reshape(-1)

    none = jnp.zeros((width,), F32)
    small = jnp.concatenate(
        [none, none, put_heads(sum_qkv[0, :part]), put_heads(sum_qkv[0, 2 * part :]), sums4[2], sums4[0], sums4[1],
         put_hidden(sum_up[0]), sums4[3]]
    ).reshape(-1, width)
    small = pad_rows(small, 16)
    grad_in, grad_a, grad_u, small = call(
        functools.partial(k6_kernel, inner, pieces, used), 5, "first_norm_back",
        [((2, local_rows, width), BF16, ANY), ((used, width), F32, VM), ((used, width), F32, VM), (small.shape, F32, VM)],
        [(grads, VM), (wa, VM), (cells, VM), (grad_mid, VM), (line(ln1_gain), VM), (small, VM),
         (part_a.reshape(slabs), VM), (line_gu, VM)],
        [pltpu.VMEM(half, F32), pltpu.VMEM(half, BF16), pltpu.VMEM(half, BF16), pltpu.VMEM(half, BF16),
         pltpu.VMEM(lines, BF16), pltpu.VMEM((6, *small.shape), F32), pltpu.VMEM((5, *small.shape), F32),
         *PlaneReduce.scratch(pieces, width), *LineReduce.scratch(pieces, width), *LineReduce.scratch(pieces, width),
         dma((2,)), dma((2,)), dma((1,)), dma((1,)), dma((1,)), dma((5,)), dma((5,))],
    )
    qkv_rows = shards[0].size // width
    grads = [grad_a[:qkv_rows], grad_a[qkv_rows:], grad_u, grad_d]
    grads = [g.reshape(s.shape) for g, s in zip(grads, shards)]
    if inner > 1:
        grads = [
            lax.psum_scatter(g, "wide", scatter_dimension=1, axis_index_groups=groups, tiled=True)
            for g in grads
        ]
    hid = bias_up.shape[0] // width
    flat = [
        small[0], small[1], small[2:4].reshape(-1), small[4], small[5], small[6],
        small[7 : 7 + hid].reshape(-1), small[7 + hid],
    ]
    return (cells_out[:, None], grad_in[:, None], *grads, *flat)


def solution(mesh):
    cell = P(None, "wide", "narrow", None)
    shard = P("narrow", "wide")
    return jax.shard_map(
        on_device,
        mesh=mesh,
        in_specs=(cell, P(None, "wide"), *[shard] * 4, *[P()] * 8, cell),
        out_specs=(cell, cell, *[shard] * 4, *[P()] * 8),
        check_vma=False,
    )
```

time: 2180 us -> 470 us (0.22)
  waiting for transfers between devices: 1410 us -> 0 us
  Pallas kernels: 0 us -> 429 us
  local copies, waits for them, and re-layouts: 308 us -> 30.4 us
  matrix products: 246 us -> 0 us
  blocking collectives: 80.8 us -> 0 us
  starting transfers between devices: 53.6 us -> 0 us
  other arithmetic: 51.9 us -> 0.84 us
    unnamed x23 -> x0, waiting for transfers between devices: 1100 us -> none
    pallas_call x0 -> x6, Pallas kernels: none -> 429 us  [call(): pl.pallas_call(kernel, out_shape=[jax.ShapeDtypeStruct(s, d) for s, d, _...]
    dot_general x48 -> x0, matrix products: 246 us -> none  [the longest x2 25.1 us: on_device(): jnp.einsum('td,fd->tf', normed2_low, up_rows, preferred_element_type=jnp....]
    all_gather x15 -> x0, waiting for transfers between devices: 165 us -> none  [the longest x1 52 us: gather_batch(): lax.all_gather(shards[0], 'wide', axis=1, tiled=True)]
    all_to_all x12 -> x0, waiting for transfers between devices: 142 us -> none  [the longest x2 46.9 us: on_device(): lax.all_to_all(hidden_low.reshape(local_rows, groups, ff_here), 'narrow',...]
    unnamed x226 -> x49, local copies, waits for them, and re-layouts: 134 us -> 9.89 us
    reshape x10 -> x24, local copies, waits for them, and re-layouts: 73.9 us -> 12 us  [the longest x8 5.59 us: line(): return v.reshape(1, -1)]
    all_to_all x12 -> x0, starting transfers between devices: 52.4 us -> none  [the longest x2 9.46 us: on_device(): lax.all_to_all(grad_upper_low.reshape(local_rows, groups, ff_here), 'narr...]
  transfers between devices with their start and end apart: 31 -> 0, of which waited for: 15 -> 0; matrix products, arithmetic and copies ran while one was open for 24% -> 0% of each run, Pallas kernels for 0% -> 0%
where the time goes in v2:
time: 470 us; the launch traced here: 462 us
  Pallas kernels  429 us (91%)
  local copies, waits for them, and re-layouts  30.4 us (6%)
    pallas_call x6, Pallas kernels, call(): pl.pallas_call(kernel, out_shape=[jax.ShapeDtypeStruct(s, d) for s, d, _...  429 us
    unnamed x49, local copies, waits for them, and re-layouts  9.89 us

profile of v2, /device:TPU:0, one launch (start us, length us, event | category | flops | bytes accessed | tf_op | source)
XLA Modules:
  0.0 461.6 jit_solution(10705582219852265105)
XLA Ops:
  0.7 0.9 fusion.3
  2.0 0.6 reshape.153.refs_4_
  3.2 1.3 reshape.145.refs_4_
  4.5 2.4 copy.42
  6.9 1.4 copy.43
  8.9 0.8 fusion.2.refs_0_
  9.7 0.8 pad.32.refs_1_
  10.5 0.6 reshape.146.refs_5_
  11.1 79.4 %gather_first.1 = (bf16[16,144,1120]{2,1,0:T(8,128)(2,1)}, bf16[4,144,1120]{2,1,0:T(8,128)(2,1)}, bf16[4,256,1120]{2,1,0:T(8,128)(2,1)}, bf16[4,256,1120]{2,1,0:T(8,128)(2,1)}, bf16[4,256,1120]{2,1,0:T(8,128)(2,1)}) custom-call(bf16[144,1120]{1,0:T(8,128)(2,1)} %fusion.2.refs_0_, bf16[144,1120]{1,0:T(8,128)(2,1)} %pad.32.refs_1_, ...), custom_call_target="tpu_custom_call" | custom-call | tf_op jit(solution)/shard_map/gather_first/pallas_call | solution.py:929
  90.5 0.6 reshape.155.refs_6_.refs_10_
  91.1 0.8 pad.35.refs_10_
  91.8 0.6 reshape.154.refs_5_
  93.0 66.3 %attend.1 = (bf16[16,144,1120]{2,1,0:T(8,128)(2,1)}, bf16[4,144,1120]{2,1,0:T(8,128)(2,1)}, bf16[1024,1920]{1,0:T(8,128)(2,1)}, bf16[1024,640]{1,0:T(8,128)(2,1)...) custom-call(bf16[2,1152,1120]{2,1,0:T(8,128)(2,1)} %bitcast.50, ...), custom_call_target="tpu_custom_call" | custom-call | tf_op jit(solution)/shard_map/attend/pallas_call | solution.py:929
  159.4 1.4 reshape.158
  161.2 0.7 reshape.159.refs_2_
  161.9 56.4 %hidden_units.1 = (bf16[16,144,1120]{2,1,0:T(8,128)(2,1)}, bf16[1024,2304]{1,0:T(8,128)(2,1)}, bf16[1024,2304]{1,0:T(8,128)(2,1)}, bf16[2304,1120]{1,0:T(8,128)(2,1)}) custom-call(bf16[1024,1120]{1,0:T(8,128)(2,1)} %get-tuple-element.52.refs_0_.refs_5_, bf16[2304,1120]{1,0:T(8,128)(2,1)} %bitcast.40, f32[1,2304]{1,0:T(1,128)} %reshape.159.refs_2_, ...), custom_call_target="tpu_custom_call" | custom-call | tf_op jit(solution)/shard_map/hidden_units/pallas_call | solution.py:929
  218.3 2.6 slice.84.refs_8_
  221.0 0.6 reshape.162.refs_9_
  221.6 73.8 %hidden_units_back.1 = (bf16[2,256,1120]{2,1,0:T(8,128)(2,1)}, bf16[4,144,1120]{2,1,0:T(8,128)(2,1)}, bf16[2304,1120]{1,0:T(8,128)(2,1)}, bf16[640,1120]{1,0:T(8...) custom-call(bf16[1024,2304]{1,0:T(8,128)(2,1)} %get-tuple-element.56.re, ...), custom_call_target="tpu_custom_call" | custom-call | tf_op jit(solution)/shard_map/hidden_units_back/pallas_call | solution.py:929
  295.4 66.4 %attend_back.1 = (bf16[1024,1920]{1,0:T(8,128)(2,1)}, bf16[2,1152,1120]{2,1,0:T(8,128)(2,1)}, bf16[4,144,1120]{2,1,0:T(8,128)(2,1)}, f32[140,1120]{1,0:T(8,128)}, f32[1,1920]{1,0:T(1,128)}) custom-call(bf16[1024,1920]{1,0:T(8,128)(2,1)} %get-tuple-element.64.refs_0_, f32[1024,128]{1,0:T(8,128)} %get-tuple-element.65.refs_1_, ...), custom_call_target="tpu_custom_call" | custom-call | tf_op jit(solution)/shard_map/attend_back/pallas_call | solution.py:929
  361.8 0.7 slice_reduce_fusion.10
  364.3 0.6 pad.37.refs_5_
  365.0 86.5 %first_norm_back.1 = (bf16[2,256,1120]{2,1,0:T(8,128)(2,1)}, f32[140,1120]{1,0:T(8,128)}, f32[140,1120]{1,0:T(8,128)}, f32[16,1120]{1,0:T(8,128)}) custom-call(bf16[1024,1920]{1,0:T(8,128)(2,1)} %get-tuple-element.70.refs_0_, bf16[2560,1120]{1,0:T(8,128)(2,1)} %get-tuple-element.61.refs_1_, bf16[4,256,1120]{2,1,0:T(8,128)(2,1)} %get-tuple-element.50.refs_3_.refs_2_, ...), custom_call_target="tpu_custom_call" | custom-call | tf_op jit(solution)/shard_map/first_norm_back/pallas_call | solution.py:929
  451.5 2.5 copy.52
  454.1 1.1 reshape.171
  455.2 0.8 reshape.172
  456.0 0.7 slice_reduce_fusion
  456.7 0.7 reshape.174
  457.4 0.7 reshape.173
  458.1 1.4 copy.51
  459.5 0.8 copy.66
  460.3 0.8 copy.67
  (81 shorter events, 4.4 us)
Async XLA Ops:
  0.6 1.9 copy-start
  0.7 6.2 %copy-start.3 = (bf16[2,1,256,1120]{2,3,1,0:T(8,128)(2,1)S(1)}, bf16[2,1,256,1120]{2,3,1,0:T(8,128)(2,1)}, u32[]{:S(2)}) copy-start(bf16[2,1,256,1120]{2,3,1,0:T(8,128)(2,1)} %param.31) | copy-start | bytes 3440644
  2.0 6.3 %copy-start.9 = (bf16[15,7840]{1,0:T(8,128)(2,1)S(1)}, bf16[15,7840]{1,0:T(8,128)(2,1)}, u32[]{:S(2)}) copy-start(bf16[15,7840]{1,0:T(8,128)(2,1)} %param.19) | copy-start | bytes 705604
  4.4 4.3 copy-start.10
  6.8 2.8 copy-start.7
  6.8 3.6 copy-start.15
  8.7 81.8 %copy-start.16 = (f32[1120]{0:T(1024)S(1)}, f32[1120]{0:T(1024)}, u32[]{:S(2)}) copy-start(f32[1120]{0:T(1024)} %param.27) | copy-start | bytes 13444
  8.7 82.4 %copy-start.8 = (bf16[140,1120]{1,0:T(8,128)(2,1)S(1)}, bf16[140,1120]{1,0:T(8,128)(2,1)}, u32[]{:S(2)}) copy-start(bf16[140,1120]{1,0:T(8,128)(2,1)} %param.22) | copy-start | bytes 940804
  9.7 82.2 %copy-start.17 = (f32[1120]{0:T(1024)S(1)}, f32[1120]{0:T(1024)}, u32[]{:S(2)}) copy-start(f32[1120]{0:T(1024)} %param.26) | copy-start | bytes 13444
  9.7 82.7 %copy-start.18 = (f32[1120]{0:T(1024)S(1)}, f32[1120]{0:T(1024)}, u32[]{:S(2)}) copy-start(f32[1120]{0:T(1024)} %param.28) | copy-start | bytes 13444
  93.0 66.3 %copy-start.12 = (f32[4480]{0:T(1024)S(1)}, f32[4480]{0:T(1024)}, u32[]{:S(2)}) copy-start(f32[4480]{0:T(1024)} %param.29) | copy-start | bytes 53764
  218.3 2.7 copy-start.19
  295.4 67.5 %copy-start.14 = (f32[1,2304]{1,0:T(1,128)S(1)}, f32[1,2304]{1,0:T(1,128)}, u32[]{:S(2)}) copy-start(f32[1,2304]{1,0:T(1,128)} %get-tuple-element.74) | copy-start | bytes 27652
  295.4 68.7 %copy-start.13 = (f32[8,1120]{1,0:T(8,128)S(1)}, f32[8,1120]{1,0:T(8,128)}, u32[]{:S(2)}) copy-start(f32[8,1120]{1,0:T(8,128)} %get-tuple-element.73) | copy-start | bytes 107524
  451.5 2.5 copy-start.4
  451.5 4.5 copy-start.11
  451.5 6.5 %copy-start.2 = (bf16[2,256,1120]{2,1,0:T(8,128)(2,1)S(1)}, bf16[2,256,1120]{2,1,0:T(8,128)(2,1)}, u32[]{:S(2)}) copy-start(bf16[2,256,1120]{2,1,0:T(8,128)(2,1)} %get-tuple-element.63) | copy-start | bytes 3440644
  454.1 5.4 %copy-start.6 = (f32[140,1120]{1,0:T(8,128)S(1)}, f32[140,1120]{1,0:T(8,128)}, u32[]{:S(2)}) copy-start(f32[140,1120]{1,0:T(8,128)} %get-tuple-element.158) | copy-start | bytes 1881604
  455.1 5.1 %copy-start.5 = (f32[140,1120]{1,0:T(8,128)S(1)}, f32[140,1120]{1,0:T(8,128)}, u32[]{:S(2)}) copy-start(f32[140,1120]{1,0:T(8,128)} %get-tuple-element.159) | copy-start | bytes 1881604
  458.1 3.1 copy-start.1
